TPU v7x, 32 devices: a whole 2x2x4 slice. The times are simulated.
32 devices in a mesh: sub: 8 (over z, y), grp: 4 (over x, core).
Axes of the slice: x: 2, y: 2, z: 4, core: 2. Of those that a mesh axis runs over, the one named last changes fastest.
Arguments:
- lam_start: float32 [32768, 128], P(('sub', 'grp')), may hold values from -6 to 6
- loads: float32 [32768, 128], P(('sub', 'grp')), may hold values from -40 to 40
- dual_ops: bfloat16 [32, 1024, 1024], P(('sub', 'grp')), may hold values from -40 to 40, as said below
- modes: float32 [6, 32768], P(None, ('sub', 'grp')), may hold values from -0.6 to 0.6
- coarse_inverse: float32 [192, 192], P('sub', 'grp'), may hold values from -1 to 1, as said below
- face_offset: int32 [8, 4, 8], P(None, 'grp'), may hold values from 0 to 3, as said below
- face_block: int32 [8, 4, 8], P(None, 'grp'), may hold values from 0 to 7
- face_sign: int32 [8, 4, 8], P(None, 'grp'), may hold values from 0 to 1
- contact: int32 [3, 32768], P(None, ('sub', 'grp')), may hold values 0 or 1
Outputs:
- multipliers: float32 [32768, 128], P(('sub', 'grp'))
Inputs may be any that keep to these rules, and one draw needn't show every extreme that they name: Each block dual_ops[k] is symmetric positive definite. coarse_inverse is symmetric positive definite. `face_offset`: no face reads from outside the order 0 to 7. For every subdomain no value is taken by more than 4 of its faces, and exactly 4 of its faces share one value.
All inputs are finite; a program needn't handle non-finite values. No bound on the sum of `contact` on one device may be relied on, other than what follows from the above.
Results may differ from a plain program's by a relative error of at most 0.005.
Values may be sent and summed in bfloat16 or wider, within the bound.
No kernel may reach another device: no remote copies, remote signals or barrier semaphores. Data moves between devices by JAX's collectives and lax.ppermute only.
A program may use at most 64 MiB of HBM per device.

v0:
```python
import jax
import jax.numpy as jnp
from jax import lax
from jax.sharding import PartitionSpec as P

FACES = 8
FACE_ROWS = 32
CAP = 4
MODES = 6
STEPS = 3


def passed_along(value, axis, steps):
    count = lax.axis_size(axis)
    leading, last = (max(0, -steps), min(count, count - steps))
    return lax.ppermute(value, axis, [(source, source + steps) for source in range(leading, last)])


def own_row(table, index):
    return lax.dynamic_index_in_dim(table[:, 0, :], index, 0, keepdims=False)


def slot_matrix(offsets, which):
    match = (offsets == which).astype(jnp.int32)
    rank = jnp.cumsum(match) - 1
    picked = (rank[:, None] == jnp.arange(CAP, dtype=jnp.int32)[None, :]) & (match[:, None] == 1)
    return picked.astype(jnp.float32)


def build_tables(face_offset, face_block, face_sign):
    sub_here = lax.axis_index("sub")
    sub_count = lax.axis_size("sub")
    offs_own = own_row(face_offset, sub_here)
    sign_own = (2 * own_row(face_sign, sub_here) - 1).astype(jnp.float32)
    block_ids = jnp.arange(FACES, dtype=jnp.int32)
    tables = []
    for which, moved in enumerate((-2, -1, 1, 2)):
        reader = jnp.clip(sub_here - moved, 0, sub_count - 1)
        offs_far = own_row(face_offset, reader)
        blocks_far = own_row(face_block, reader)
        sign_far = (2 * own_row(face_sign, reader) - 1).astype(jnp.float32)
        onehot_far = (blocks_far[:, None] == block_ids[None, :]).astype(jnp.float32)
        sel_own = slot_matrix(offs_own, which)
        sel_far = slot_matrix(offs_far, which)
        pack = jnp.dot(sel_far.T, onehot_far).astype(jnp.bfloat16)
        place = (sel_own * sign_own[:, None]).astype(jnp.bfloat16)
        unpack = jnp.dot((sel_far * sign_far[:, None]).T, onehot_far).astype(jnp.bfloat16)
        tables.append((moved, pack, place, sel_own.astype(jnp.bfloat16), unpack))
    return tables


def apply_dual(field, dual_ops, tables):
    normal_loads = field.shape[-1]
    face_total = FACES * FACE_ROWS
    low = field.astype(jnp.bfloat16)
    faces = low[:face_total].reshape(FACES, FACE_ROWS, normal_loads)
    gathered = faces.astype(jnp.float32)
    for moved, pack, place, sel_own, unpack in tables:
        outgoing = jnp.einsum(
            "jb,brl->jrl", pack, faces, preferred_element_type=jnp.float32
        ).astype(jnp.bfloat16)
        arrived = passed_along(outgoing, "sub", -moved)
        gathered = gathered + jnp.einsum(
            "fj,jrl->frl", place, arrived, preferred_element_type=jnp.float32
        )
    zfull = jnp.concatenate(
        [gathered.astype(jnp.bfloat16).reshape(face_total, normal_loads), low[face_total:]], axis=0
    )
    image = jnp.dot(dual_ops[0], zfull, preferred_element_type=jnp.float32).astype(jnp.bfloat16)
    yfaces = image[:face_total].reshape(FACES, FACE_ROWS, normal_loads)
    returned = jnp.zeros((FACES, FACE_ROWS, normal_loads), jnp.float32)
    for moved, pack, place, sel_own, unpack in tables:
        leaving = jnp.einsum(
            "fj,frl->jrl", sel_own, yfaces, preferred_element_type=jnp.float32
        ).astype(jnp.bfloat16)
        coming = passed_along(leaving, "sub", moved)
        returned = returned + jnp.einsum(
            "jb,jrl->brl", unpack, coming, preferred_element_type=jnp.float32
        )
    result = image.astype(jnp.float32)
    return jnp.concatenate(
        [result[:face_total] + returned.reshape(face_total, normal_loads), result[face_total:]],
        axis=0,
    )


def inverse_own_rows(coarse_inverse):
    full_rows = lax.all_gather(coarse_inverse, "grp", axis=1, tiled=True)
    return lax.dynamic_slice_in_dim(full_rows, lax.axis_index("grp") * MODES, MODES, 0)


def coarse_direction(dual_gradient, modes, own_inverse):
    residual = jnp.dot(
        modes, dual_gradient, precision=lax.Precision.HIGHEST, preferred_element_type=jnp.float32
    )
    every_res = lax.all_gather(residual, ("sub", "grp"), axis=0, tiled=True)
    own_corr = jnp.dot(
        own_inverse, every_res, precision=lax.Precision.HIGHEST, preferred_element_type=jnp.float32
    )
    return dual_gradient - jnp.einsum("mr,ml->rl", modes, own_corr, precision=lax.Precision.HIGHEST)


def on_device(
    lam_start, loads, dual_ops, modes, coarse_inverse, face_offset, face_block, face_sign, contact
):
    tables = build_tables(face_offset, face_block, face_sign)
    own_inverse = inverse_own_rows(coarse_inverse)
    lam = lam_start
    for step in range(STEPS):
        dual_gradient = apply_dual(lam, dual_ops, tables) - loads
        search_direction = coarse_direction(dual_gradient, modes, own_inverse)
        local_slope = jnp.sum(dual_gradient * search_direction, axis=0)
        slope = lax.psum(local_slope, ("sub", "grp"))
        image = apply_dual(search_direction, dual_ops, tables)
        curv = lax.psum(jnp.sum(search_direction * image, axis=0), ("sub", "grp"))
        alpha = slope / curv
        lam = lam - alpha[None, :] * search_direction
        active = contact[step][:, None] == 1
        lam = jnp.where(active, jnp.maximum(lam, 0.0), lam)
    return lam


def solution(mesh):
    return jax.shard_map(
        on_device,
        mesh=mesh,
        in_specs=(
            P(("sub", "grp"), None),
            P(("sub", "grp"), None),
            P(("sub", "grp"), None, None),
            P(None, ("sub", "grp")),
            P("sub", "grp"),
            P(None, "grp", None),
            P(None, "grp", None),
            P(None, "grp", None),
            P(None, ("sub", "grp")),
        ),
        out_specs=P(("sub", "grp"), None),
        check_vma=False,
    )
```

profile of v0, /device:TPU:0, one launch (start us, length us, event | category | flops | bytes accessed | tf_op | source)
XLA Modules:
  0.0 566.3 jit_solution(1420211075383612907)
XLA Ops:
  8.7 5.5 collective-permute-start.1
  15.3 4.6 collective-permute-start
  26.2 5.2 all-gather
  39.3 7.5 %collective-permute-start.7 = (bf16[4,32,128]{2,0,1:T(4,128)(2,1)S(1)}, bf16[4,32,128]{2,0,1:T(4,128)(2,1)S(1)}, u32[]{:S(2)}, u32[]{:S(2)}) collective-permute-start(bf16[4,32,128]{2,0,1:T(4,128)(2,1)S(1)} %convolution_convert_fusion.40), channel_id=1, source_target_pairs={{0,8},{4,12},{8,16},{12,20},{16,24},{20,28},{1,9},{5,13},{9,17},{1... | collective-permute-start | bytes 98312 | tf_op jit(solution)/shard_map/ppermute | solution.py:16
  46.8 2.5 collective-permute-start.6
  55.7 40.6 %all-gather.1 = f32[32,6,128]{2,1,0:T(8,128)S(1)} all-gather(f32[1,6,128]{2,1,0:T(8,128)S(1)} %convolution_bitcast_fusion.5), channel_id=1, replica_groups=mesh['sub'=8,'grp'=4] {'sub','grp'}, dimensions={0}, use_global_device_ids=true | all-gather | bytes 101376 | tf_op jit(solution)/shard_map/all_gather | solution.py:96
  111.1 5.2 collective-permute-start.8
  121.2 2.6 fusion.293
  134.9 6.6 %collective-permute-start.15 = (bf16[4,32,128]{2,0,1:T(4,128)(2,1)S(1)}, bf16[4,32,128]{2,0,1:T(4,128)(2,1)S(1)}, u32[]{:S(2)}, u32[]{:S(2)}) collective-permute-start(bf16[4,32,128]{2,0,1:T(4,128)(2,1)S(1)} %convolution_convert_fusion.32), channel_id=1, source_target_pairs={{0,8},{4,12},{8,16},{12,20},{16,24},{20,28},{1,9},{5,13},{9,17},{1... | collective-permute-start | bytes 98312 | tf_op jit(solution)/shard_map/ppermute | solution.py:16
  141.5 2.8 collective-permute-start.14
  153.6 43.3 %all-reduce.2 = (f32[128]{0:T(128)S(1)}, f32[128]{0:T(128)S(1)}) all-reduce(f32[128]{0:T(128)} %get-tuple-element.10, f32[128]{0:T(128)} %get-tuple-element.9), channel_id=1, replica_groups=mesh['sub'=8,'grp'=4] {'sub','grp'}, use_global_device_ids=true, to_apply=%region_9.10 | all-reduce | flops 256 | bytes 2048 | tf_op jit(solution)/shard_map/psum | solution.py:113
  200.6 4.2 collective-permute-start.17
  208.9 5.2 collective-permute-start.16
  216.0 2.6 fusion.294
  223.7 6.6 %collective-permute-start.23 = (bf16[4,32,128]{2,0,1:T(4,128)(2,1)S(1)}, bf16[4,32,128]{2,0,1:T(4,128)(2,1)S(1)}, u32[]{:S(2)}, u32[]{:S(2)}) collective-permute-start(bf16[4,32,128]{2,0,1:T(4,128)(2,1)S(1)} %convolution_convert_fusion.24), channel_id=1, source_target_pairs={{0,8},{4,12},{8,16},{12,20},{16,24},{20,28},{1,9},{5,13},{9,17},{1... | collective-permute-start | bytes 98312 | tf_op jit(solution)/shard_map/ppermute | solution.py:16
  230.3 2.8 collective-permute-start.22
  242.5 43.8 %all-gather.2 = f32[32,6,128]{2,1,0:T(8,128)} all-gather(f32[1,6,128]{2,1,0:T(8,128)S(1)} %convolution_bitcast_fusion.4), channel_id=1, replica_groups=mesh['sub'=8,'grp'=4] {'sub','grp'}, dimensions={0}, use_global_device_ids=true | all-gather | bytes 101376 | tf_op jit(solution)/shard_map/all_gather | solution.py:96
  303.7 5.2 collective-permute-start.24
  313.7 2.5 fusion.296
  327.4 6.6 %collective-permute-start.31 = (bf16[4,32,128]{2,0,1:T(4,128)(2,1)S(1)}, bf16[4,32,128]{2,0,1:T(4,128)(2,1)S(1)}, u32[]{:S(2)}, u32[]{:S(2)}) collective-permute-start(bf16[4,32,128]{2,0,1:T(4,128)(2,1)S(1)} %convolution_convert_fusion.16), channel_id=1, source_target_pairs={{0,8},{4,12},{8,16},{12,20},{16,24},{20,28},{1,9},{5,13},{9,17},{1... | collective-permute-start | bytes 98312 | tf_op jit(solution)/shard_map/ppermute | solution.py:16
  334.0 2.8 collective-permute-start.30
  346.1 43.3 %all-reduce.1 = (f32[128]{0:T(128)S(1)}, f32[128]{0:T(128)S(1)}) all-reduce(f32[128]{0:T(128)} %get-tuple-element.8, f32[128]{0:T(128)} %get-tuple-element.7), channel_id=1, replica_groups=mesh['sub'=8,'grp'=4] {'sub','grp'}, use_global_device_ids=true, to_apply=%region_13.14 | all-reduce | flops 256 | bytes 2048 | tf_op jit(solution)/shard_map/psum | solution.py:113
  392.3 4.2 collective-permute-start.33
  399.2 5.2 collective-permute-start.32
  411.5 6.6 %collective-permute-start.39 = (bf16[4,32,128]{2,0,1:T(4,128)(2,1)S(1)}, bf16[4,32,128]{2,0,1:T(4,128)(2,1)S(1)}, u32[]{:S(2)}, u32[]{:S(2)}) collective-permute-start(bf16[4,32,128]{2,0,1:T(4,128)(2,1)S(1)} %convolution_convert_fusion.8), channel_id=1, source_target_pairs={{0,8},{4,12},{8,16},{12,20},{16,24},{20,28},{1,9},{5,13},{9,17},{1... | collective-permute-start | bytes 98312 | tf_op jit(solution)/shard_map/ppermute | solution.py:16
  418.1 2.8 collective-permute-start.38
  425.3 40.9 %all-gather.3 = f32[32,6,128]{2,1,0:T(8,128)S(1)} all-gather(f32[1,6,128]{2,1,0:T(8,128)S(1)} %convolution_bitcast_fusion.3), channel_id=1, replica_groups=mesh['sub'=8,'grp'=4] {'sub','grp'}, dimensions={0}, use_global_device_ids=true | all-gather | bytes 101376 | tf_op jit(solution)/shard_map/all_gather | solution.py:96
  481.2 5.2 collective-permute-start.40
  491.2 2.6 fusion.299
  504.9 6.6 %collective-permute-start.47 = (bf16[4,32,128]{2,0,1:T(4,128)(2,1)S(1)}, bf16[4,32,128]{2,0,1:T(4,128)(2,1)S(1)}, u32[]{:S(2)}, u32[]{:S(2)}) collective-permute-start(bf16[4,32,128]{2,0,1:T(4,128)(2,1)S(1)} %convolution_convert_fusion), channel_id=1, source_target_pairs={{0,8},{4,12},{8,16},{12,20},{16,24},{20,28},{1,9},{5,13},{9,17},{1... | collective-permute-start | bytes 98312 | tf_op jit(solution)/shard_map/ppermute | solution.py:16
  511.6 2.8 collective-permute-start.46
  521.1 43.0 %all-reduce = (f32[128]{0:T(128)S(1)}, f32[128]{0:T(128)S(1)}) all-reduce(f32[128]{0:T(128)S(1)} %get-tuple-element.6, f32[128]{0:T(128)S(1)} %get-tuple-element.5), channel_id=1, replica_groups=mesh['sub'=8,'grp'=4] {'sub','grp'}, use_global_device_ids=true, to_apply=%region_17.18 | all-reduce | flops 256 | bytes 2048 | tf_op jit(solution)/shard_map/psum | solution.py:113
  (403 shorter events, 193.2 us)
Async XLA Ops:
  3.9 29.8 %collective-permute-start.3 = (bf16[4,32,128]{2,0,1:T(4,128)(2,1)S(1)}, bf16[4,32,128]{2,0,1:T(4,128)(2,1)S(1)}, u32[]{:S(2)}, u32[]{:S(2)}) collective-permute-start(bf16[4,32,128]{2,0,1:T(4,128)(2,1)S(1)} %convolution_convert_fusion.44), channel_id=1, source_target_pairs={{8,0},{12,4},{16,8},{20,12},{24,16},{28,20},{9,1},{13,5},{17,9},{2... | collective-permute-start | bytes 98312 | tf_op jit(solution)/shard_map/ppermute | solution.py:16
  6.3 27.3 %collective-permute-start.2 = (bf16[4,32,128]{2,0,1:T(4,128)(2,1)S(1)}, bf16[4,32,128]{2,0,1:T(4,128)(2,1)S(1)}, u32[]{:S(2)}, u32[]{:S(2)}) collective-permute-start(bf16[4,32,128]{2,0,1:T(4,128)(2,1)S(1)} %convolution_convert_fusion.45), channel_id=1, source_target_pairs={{4,0},{8,4},{12,8},{16,12},{20,16},{24,20},{28,24},{5,1},{9,5},{13... | collective-permute-start | bytes 98312 | tf_op jit(solution)/shard_map/ppermute | solution.py:16
  8.7 24.6 %collective-permute-start.1 = (bf16[4,32,128]{2,0,1:T(4,128)(2,1)S(1)}, bf16[4,32,128]{2,0,1:T(4,128)(2,1)S(1)}, u32[]{:S(2)}, u32[]{:S(2)}) collective-permute-start(bf16[4,32,128]{2,0,1:T(4,128)(2,1)S(1)} %convolution_convert_fusion.46), channel_id=1, source_target_pairs={{0,4},{4,8},{8,12},{12,16},{16,20},{20,24},{24,28},{1,5},{5,9},{9,... | collective-permute-start | bytes 98312 | tf_op jit(solution)/shard_map/ppermute | solution.py:16
  15.3 18.7 %collective-permute-start = (bf16[4,32,128]{2,0,1:T(4,128)(2,1)S(1)}, bf16[4,32,128]{2,0,1:T(4,128)(2,1)S(1)}, u32[]{:S(2)}, u32[]{:S(2)}) collective-permute-start(bf16[4,32,128]{2,0,1:T(4,128)(2,1)S(1)} %convolution_convert_fusion.47), channel_id=1, source_target_pairs={{0,8},{4,12},{8,16},{12,20},{16,24},{20,28},{1,9},{5,13},{9,17},{1... | collective-permute-start | bytes 98312 | tf_op jit(solution)/shard_map/ppermute | solution.py:16
  36.5 12.8 %collective-permute-start.5 = (bf16[4,32,128]{2,0,1:T(4,128)(2,1)S(1)}, bf16[4,32,128]{2,0,1:T(4,128)(2,1)S(1)}, u32[]{:S(2)}, u32[]{:S(2)}) collective-permute-start(bf16[4,32,128]{2,0,1:T(4,128)(2,1)S(1)} %convolution_convert_fusion.42), channel_id=1, source_target_pairs={{4,0},{8,4},{12,8},{16,12},{20,16},{24,20},{28,24},{5,1},{9,5},{13... | collective-permute-start | bytes 98312 | tf_op jit(solution)/shard_map/ppermute | solution.py:16
  38.0 14.6 %collective-permute-start.4 = (bf16[4,32,128]{2,0,1:T(4,128)(2,1)S(1)}, bf16[4,32,128]{2,0,1:T(4,128)(2,1)S(1)}, u32[]{:S(2)}, u32[]{:S(2)}) collective-permute-start(bf16[4,32,128]{2,0,1:T(4,128)(2,1)S(1)} %convolution_convert_fusion.43), channel_id=1, source_target_pairs={{8,0},{12,4},{16,8},{20,12},{24,16},{28,20},{9,1},{13,5},{17,9},{2... | collective-permute-start | bytes 98312 | tf_op jit(solution)/shard_map/ppermute | solution.py:16
  39.3 12.4 %collective-permute-start.7 = (bf16[4,32,128]{2,0,1:T(4,128)(2,1)S(1)}, bf16[4,32,128]{2,0,1:T(4,128)(2,1)S(1)}, u32[]{:S(2)}, u32[]{:S(2)}) collective-permute-start(bf16[4,32,128]{2,0,1:T(4,128)(2,1)S(1)} %convolution_convert_fusion.40), channel_id=1, source_target_pairs={{0,8},{4,12},{8,16},{12,20},{16,24},{20,28},{1,9},{5,13},{9,17},{1... | collective-permute-start | bytes 98312 | tf_op jit(solution)/shard_map/ppermute | solution.py:16
  104.7 11.7 %collective-permute-start.9 = (bf16[4,32,128]{2,0,1:T(4,128)(2,1)S(1)}, bf16[4,32,128]{2,0,1:T(4,128)(2,1)S(1)}, u32[]{:S(2)}, u32[]{:S(2)}) collective-permute-start(bf16[4,32,128]{2,0,1:T(4,128)(2,1)S(1)} %convolution_convert_fusion.38), channel_id=1, source_target_pairs={{0,4},{4,8},{8,12},{12,16},{16,20},{20,24},{24,28},{1,5},{5,9},{9,... | collective-permute-start | bytes 98312 | tf_op jit(solution)/shard_map/ppermute | solution.py:16
  108.6 8.2 %collective-permute-start.11 = (bf16[4,32,128]{2,0,1:T(4,128)(2,1)S(1)}, bf16[4,32,128]{2,0,1:T(4,128)(2,1)S(1)}, u32[]{:S(2)}, u32[]{:S(2)}) collective-permute-start(bf16[4,32,128]{2,0,1:T(4,128)(2,1)S(1)} %convolution_convert_fusion.36), channel_id=1, source_target_pairs={{8,0},{12,4},{16,8},{20,12},{24,16},{28,20},{9,1},{13,5},{17,9},{2... | collective-permute-start | bytes 98312 | tf_op jit(solution)/shard_map/ppermute | solution.py:16
  129.6 14.7 %collective-permute-start.13 = (bf16[4,32,128]{2,0,1:T(4,128)(2,1)S(1)}, bf16[4,32,128]{2,0,1:T(4,128)(2,1)S(1)}, u32[]{:S(2)}, u32[]{:S(2)}) collective-permute-start(bf16[4,32,128]{2,0,1:T(4,128)(2,1)S(1)} %convolution_convert_fusion.34), channel_id=1, source_target_pairs={{4,0},{8,4},{12,8},{16,12},{20,16},{24,20},{28,24},{5,1},{9,5},{13... | collective-permute-start | bytes 98312 | tf_op jit(solution)/shard_map/ppermute | solution.py:16
  133.6 14.0 %collective-permute-start.12 = (bf16[4,32,128]{2,0,1:T(4,128)(2,1)S(1)}, bf16[4,32,128]{2,0,1:T(4,128)(2,1)S(1)}, u32[]{:S(2)}, u32[]{:S(2)}) collective-permute-start(bf16[4,32,128]{2,0,1:T(4,128)(2,1)S(1)} %convolution_convert_fusion.35), channel_id=1, source_target_pairs={{8,0},{12,4},{16,8},{20,12},{24,16},{28,20},{9,1},{13,5},{17,9},{2... | collective-permute-start | bytes 98312 | tf_op jit(solution)/shard_map/ppermute | solution.py:16
  134.9 11.9 %collective-permute-start.15 = (bf16[4,32,128]{2,0,1:T(4,128)(2,1)S(1)}, bf16[4,32,128]{2,0,1:T(4,128)(2,1)S(1)}, u32[]{:S(2)}, u32[]{:S(2)}) collective-permute-start(bf16[4,32,128]{2,0,1:T(4,128)(2,1)S(1)} %convolution_convert_fusion.32), channel_id=1, source_target_pairs={{0,8},{4,12},{8,16},{12,20},{16,24},{20,28},{1,9},{5,13},{9,17},{1... | collective-permute-start | bytes 98312 | tf_op jit(solution)/shard_map/ppermute | solution.py:16
  200.6 13.5 %collective-permute-start.17 = (bf16[4,32,128]{2,0,1:T(4,128)(2,1)S(1)}, bf16[4,32,128]{2,0,1:T(4,128)(2,1)S(1)}, u32[]{:S(2)}, u32[]{:S(2)}) collective-permute-start(bf16[4,32,128]{2,0,1:T(4,128)(2,1)S(1)} %convolution_convert_fusion.30), channel_id=1, source_target_pairs={{0,4},{4,8},{8,12},{12,16},{16,20},{20,24},{24,28},{1,5},{5,9},{9,... | collective-permute-start | bytes 98312 | tf_op jit(solution)/shard_map/ppermute | solution.py:16
  206.3 8.2 %collective-permute-start.19 = (bf16[4,32,128]{2,0,1:T(4,128)(2,1)S(1)}, bf16[4,32,128]{2,0,1:T(4,128)(2,1)S(1)}, u32[]{:S(2)}, u32[]{:S(2)}) collective-permute-start(bf16[4,32,128]{2,0,1:T(4,128)(2,1)S(1)} %convolution_convert_fusion.28), channel_id=1, source_target_pairs={{8,0},{12,4},{16,8},{20,12},{24,16},{28,20},{9,1},{13,5},{17,9},{2... | collective-permute-start | bytes 98312 | tf_op jit(solution)/shard_map/ppermute | solution.py:16
  219.9 13.1 %collective-permute-start.21 = (bf16[4,32,128]{2,0,1:T(4,128)(2,1)S(1)}, bf16[4,32,128]{2,0,1:T(4,128)(2,1)S(1)}, u32[]{:S(2)}, u32[]{:S(2)}) collective-permute-start(bf16[4,32,128]{2,0,1:T(4,128)(2,1)S(1)} %convolution_convert_fusion.26), channel_id=1, source_target_pairs={{4,0},{8,4},{12,8},{16,12},{20,16},{24,20},{28,24},{5,1},{9,5},{13... | collective-permute-start | bytes 98312 | tf_op jit(solution)/shard_map/ppermute | solution.py:16
  222.4 14.0 %collective-permute-start.20 = (bf16[4,32,128]{2,0,1:T(4,128)(2,1)S(1)}, bf16[4,32,128]{2,0,1:T(4,128)(2,1)S(1)}, u32[]{:S(2)}, u32[]{:S(2)}) collective-permute-start(bf16[4,32,128]{2,0,1:T(4,128)(2,1)S(1)} %convolution_convert_fusion.27), channel_id=1, source_target_pairs={{8,0},{12,4},{16,8},{20,12},{24,16},{28,20},{9,1},{13,5},{17,9},{2... | collective-permute-start | bytes 98312 | tf_op jit(solution)/shard_map/ppermute | solution.py:16
  223.7 11.9 %collective-permute-start.23 = (bf16[4,32,128]{2,0,1:T(4,128)(2,1)S(1)}, bf16[4,32,128]{2,0,1:T(4,128)(2,1)S(1)}, u32[]{:S(2)}, u32[]{:S(2)}) collective-permute-start(bf16[4,32,128]{2,0,1:T(4,128)(2,1)S(1)} %convolution_convert_fusion.24), channel_id=1, source_target_pairs={{0,8},{4,12},{8,16},{12,20},{16,24},{20,28},{1,9},{5,13},{9,17},{1... | collective-permute-start | bytes 98312 | tf_op jit(solution)/shard_map/ppermute | solution.py:16
  297.2 11.7 %collective-permute-start.25 = (bf16[4,32,128]{2,0,1:T(4,128)(2,1)S(1)}, bf16[4,32,128]{2,0,1:T(4,128)(2,1)S(1)}, u32[]{:S(2)}, u32[]{:S(2)}) collective-permute-start(bf16[4,32,128]{2,0,1:T(4,128)(2,1)S(1)} %convolution_convert_fusion.22), channel_id=1, source_target_pairs={{0,4},{4,8},{8,12},{12,16},{16,20},{20,24},{24,28},{1,5},{5,9},{9,... | collective-permute-start | bytes 98312 | tf_op jit(solution)/shard_map/ppermute | solution.py:16
  301.1 8.2 %collective-permute-start.27 = (bf16[4,32,128]{2,0,1:T(4,128)(2,1)S(1)}, bf16[4,32,128]{2,0,1:T(4,128)(2,1)S(1)}, u32[]{:S(2)}, u32[]{:S(2)}) collective-permute-start(bf16[4,32,128]{2,0,1:T(4,128)(2,1)S(1)} %convolution_convert_fusion.20), channel_id=1, source_target_pairs={{8,0},{12,4},{16,8},{20,12},{24,16},{28,20},{9,1},{13,5},{17,9},{2... | collective-permute-start | bytes 98312 | tf_op jit(solution)/shard_map/ppermute | solution.py:16
  322.1 14.7 %collective-permute-start.29 = (bf16[4,32,128]{2,0,1:T(4,128)(2,1)S(1)}, bf16[4,32,128]{2,0,1:T(4,128)(2,1)S(1)}, u32[]{:S(2)}, u32[]{:S(2)}) collective-permute-start(bf16[4,32,128]{2,0,1:T(4,128)(2,1)S(1)} %convolution_convert_fusion.18), channel_id=1, source_target_pairs={{4,0},{8,4},{12,8},{16,12},{20,16},{24,20},{28,24},{5,1},{9,5},{13... | collective-permute-start | bytes 98312 | tf_op jit(solution)/shard_map/ppermute | solution.py:16
  326.1 14.0 %collective-permute-start.28 = (bf16[4,32,128]{2,0,1:T(4,128)(2,1)S(1)}, bf16[4,32,128]{2,0,1:T(4,128)(2,1)S(1)}, u32[]{:S(2)}, u32[]{:S(2)}) collective-permute-start(bf16[4,32,128]{2,0,1:T(4,128)(2,1)S(1)} %convolution_convert_fusion.19), channel_id=1, source_target_pairs={{8,0},{12,4},{16,8},{20,12},{24,16},{28,20},{9,1},{13,5},{17,9},{2... | collective-permute-start | bytes 98312 | tf_op jit(solution)/shard_map/ppermute | solution.py:16
  327.4 11.9 %collective-permute-start.31 = (bf16[4,32,128]{2,0,1:T(4,128)(2,1)S(1)}, bf16[4,32,128]{2,0,1:T(4,128)(2,1)S(1)}, u32[]{:S(2)}, u32[]{:S(2)}) collective-permute-start(bf16[4,32,128]{2,0,1:T(4,128)(2,1)S(1)} %convolution_convert_fusion.16), channel_id=1, source_target_pairs={{0,8},{4,12},{8,16},{12,20},{16,24},{20,28},{1,9},{5,13},{9,17},{1... | collective-permute-start | bytes 98312 | tf_op jit(solution)/shard_map/ppermute | solution.py:16
  392.3 12.1 %collective-permute-start.33 = (bf16[4,32,128]{2,0,1:T(4,128)(2,1)S(1)}, bf16[4,32,128]{2,0,1:T(4,128)(2,1)S(1)}, u32[]{:S(2)}, u32[]{:S(2)}) collective-permute-start(bf16[4,32,128]{2,0,1:T(4,128)(2,1)S(1)} %convolution_convert_fusion.14), channel_id=1, source_target_pairs={{0,4},{4,8},{8,12},{12,16},{16,20},{20,24},{24,28},{1,5},{5,9},{9,... | collective-permute-start | bytes 98312 | tf_op jit(solution)/shard_map/ppermute | solution.py:16
  396.6 8.2 %collective-permute-start.35 = (bf16[4,32,128]{2,0,1:T(4,128)(2,1)S(1)}, bf16[4,32,128]{2,0,1:T(4,128)(2,1)S(1)}, u32[]{:S(2)}, u32[]{:S(2)}) collective-permute-start(bf16[4,32,128]{2,0,1:T(4,128)(2,1)S(1)} %convolution_convert_fusion.12), channel_id=1, source_target_pairs={{8,0},{12,4},{16,8},{20,12},{24,16},{28,20},{9,1},{13,5},{17,9},{2... | collective-permute-start | bytes 98312 | tf_op jit(solution)/shard_map/ppermute | solution.py:16
  408.7 12.2 %collective-permute-start.37 = (bf16[4,32,128]{2,0,1:T(4,128)(2,1)S(1)}, bf16[4,32,128]{2,0,1:T(4,128)(2,1)S(1)}, u32[]{:S(2)}, u32[]{:S(2)}) collective-permute-start(bf16[4,32,128]{2,0,1:T(4,128)(2,1)S(1)} %convolution_convert_fusion.10), channel_id=1, source_target_pairs={{4,0},{8,4},{12,8},{16,12},{20,16},{24,20},{28,24},{5,1},{9,5},{13... | collective-permute-start | bytes 98312 | tf_op jit(solution)/shard_map/ppermute | solution.py:16
  410.2 12.7 %collective-permute-start.36 = (bf16[4,32,128]{2,0,1:T(4,128)(2,1)S(1)}, bf16[4,32,128]{2,0,1:T(4,128)(2,1)S(1)}, u32[]{:S(2)}, u32[]{:S(2)}) collective-permute-start(bf16[4,32,128]{2,0,1:T(4,128)(2,1)S(1)} %convolution_convert_fusion.11), channel_id=1, source_target_pairs={{8,0},{12,4},{16,8},{20,12},{24,16},{28,20},{9,1},{13,5},{17,9},{2... | collective-permute-start | bytes 98312 | tf_op jit(solution)/shard_map/ppermute | solution.py:16
  411.5 11.2 %collective-permute-start.39 = (bf16[4,32,128]{2,0,1:T(4,128)(2,1)S(1)}, bf16[4,32,128]{2,0,1:T(4,128)(2,1)S(1)}, u32[]{:S(2)}, u32[]{:S(2)}) collective-permute-start(bf16[4,32,128]{2,0,1:T(4,128)(2,1)S(1)} %convolution_convert_fusion.8), channel_id=1, source_target_pairs={{0,8},{4,12},{8,16},{12,20},{16,24},{20,28},{1,9},{5,13},{9,17},{1... | collective-permute-start | bytes 98312 | tf_op jit(solution)/shard_map/ppermute | solution.py:16
  474.7 11.7 %collective-permute-start.41 = (bf16[4,32,128]{2,0,1:T(4,128)(2,1)S(1)}, bf16[4,32,128]{2,0,1:T(4,128)(2,1)S(1)}, u32[]{:S(2)}, u32[]{:S(2)}) collective-permute-start(bf16[4,32,128]{2,0,1:T(4,128)(2,1)S(1)} %convolution_convert_fusion.6), channel_id=1, source_target_pairs={{0,4},{4,8},{8,12},{12,16},{16,20},{20,24},{24,28},{1,5},{5,9},{9,... | collective-permute-start | bytes 98312 | tf_op jit(solution)/shard_map/ppermute | solution.py:16
  478.6 8.2 %collective-permute-start.43 = (bf16[4,32,128]{2,0,1:T(4,128)(2,1)S(1)}, bf16[4,32,128]{2,0,1:T(4,128)(2,1)S(1)}, u32[]{:S(2)}, u32[]{:S(2)}) collective-permute-start(bf16[4,32,128]{2,0,1:T(4,128)(2,1)S(1)} %convolution_convert_fusion.4), channel_id=1, source_target_pairs={{8,0},{12,4},{16,8},{20,12},{24,16},{28,20},{9,1},{13,5},{17,9},{2... | collective-permute-start | bytes 98312 | tf_op jit(solution)/shard_map/ppermute | solution.py:16
  499.7 14.7 %collective-permute-start.45 = (bf16[4,32,128]{2,0,1:T(4,128)(2,1)S(1)}, bf16[4,32,128]{2,0,1:T(4,128)(2,1)S(1)}, u32[]{:S(2)}, u32[]{:S(2)}) collective-permute-start(bf16[4,32,128]{2,0,1:T(4,128)(2,1)S(1)} %convolution_convert_fusion.2), channel_id=1, source_target_pairs={{4,0},{8,4},{12,8},{16,12},{20,16},{24,20},{28,24},{5,1},{9,5},{13... | collective-permute-start | bytes 98312 | tf_op jit(solution)/shard_map/ppermute | solution.py:16
  503.7 12.7 %collective-permute-start.44 = (bf16[4,32,128]{2,0,1:T(4,128)(2,1)S(1)}, bf16[4,32,128]{2,0,1:T(4,128)(2,1)S(1)}, u32[]{:S(2)}, u32[]{:S(2)}) collective-permute-start(bf16[4,32,128]{2,0,1:T(4,128)(2,1)S(1)} %convolution_convert_fusion.3), channel_id=1, source_target_pairs={{8,0},{12,4},{16,8},{20,12},{24,16},{28,20},{9,1},{13,5},{17,9},{2... | collective-permute-start | bytes 98312 | tf_op jit(solution)/shard_map/ppermute | solution.py:16
  504.9 11.2 %collective-permute-start.47 = (bf16[4,32,128]{2,0,1:T(4,128)(2,1)S(1)}, bf16[4,32,128]{2,0,1:T(4,128)(2,1)S(1)}, u32[]{:S(2)}, u32[]{:S(2)}) collective-permute-start(bf16[4,32,128]{2,0,1:T(4,128)(2,1)S(1)} %convolution_convert_fusion), channel_id=1, source_target_pairs={{0,8},{4,12},{8,16},{12,20},{16,24},{20,28},{1,9},{5,13},{9,17},{1... | collective-permute-start | bytes 98312 | tf_op jit(solution)/shard_map/ppermute | solution.py:16
  (72 other events, 765.3 us)
where the time goes:
time: 571 us; the launch traced here: 566 us
  blocking collectives  260 us (46%)
  starting transfers between devices  136 us (24%)
  matrix products  80.8 us (14%)
  local copies, waits for them, and re-layouts  56.6 us (10%)
  other arithmetic  21 us (4%)
  waiting for transfers between devices  10.3 us (2%)
    ppermute x48, starting transfers between devices, passed_along(): lax.ppermute(value, axis, [(source, source + steps) for source in range(l...  136 us
    psum x3, blocking collectives, on_device(): slope = lax.psum(local_slope, ('sub', 'grp'))  130 us
    all_gather x3, blocking collectives, coarse_direction(): every_res = lax.all_gather(residual, ('sub', 'grp'), axis=0, tiled=True)  125 us
    dot_general x24, matrix products, apply_dual(): jnp.einsum('jb,brl->jrl', pack, faces, preferred_element_type=jnp.float32)  16.3 us
    dot_general x24, matrix products, apply_dual(): jnp.einsum('jb,jrl->brl', unpack, coming, preferred_element_type=jnp.floa...  15.2 us
    unnamed x118, local copies, waits for them, and re-layouts  13.8 us
    dot_general x24, matrix products, apply_dual(): jnp.einsum('fj,frl->jrl', sel_own, yfaces, preferred_element_type=jnp.flo...  13.7 us
    dot_general x6, matrix products, apply_dual(): jnp.dot(dual_ops[0], zfull, preferred_element_type=jnp.float32)  13.5 us
  transfers between devices with their start and end apart: 48, of which 11 were waited for; matrix products, arithmetic and copies ran while one was open for 8% of the time, Pallas kernels for 0%

commit v1 on v0

v1 whole, which is shorter than its diff:
```python
import functools

import jax
import jax.numpy as jnp
from jax import lax
from jax.experimental import pallas as pl
from jax.experimental.pallas import tpu as pltpu
from jax.sharding import PartitionSpec as P

CAP = 4
FACE_ROWS = 32
OFFSETS = (-2, -1, 1, 2)
REACH = ((2, 1), (2, 0), (1, 1), (1, 0))
SWAPS = len(REACH)
DIRECT = (1, 2, 0, 3)
SENDS = ((0, 2), (1, 2), (3,))
PAD = 8
GROUP = 3 * PAD
CONTACT_LANE = GROUP * (1 + len(OFFSETS))
SIDE = 32
FIRST_ROWS = (2 * CAP + 1) * FACE_ROWS
HALF = 64
NEAR = (0, -2, -1, 1, 2)
COARSE = -(-len(NEAR) * PAD // 16) * 16

F32 = jnp.float32
BF16 = jnp.bfloat16


def split(value):
    high = value.astype(BF16)
    return high, (value - high.astype(F32)).astype(BF16)


def partner_of(swap, position, count):
    reach, looks = REACH[swap]
    forward = lax.rem(lax.div(position, reach), 2) == looks
    partner = jnp.where(forward, position + reach, position - reach)
    which = jnp.where(forward, 2 if reach == 1 else 3, 1 if reach == 1 else 0)
    valid = (partner >= 0) & (partner < count)
    return which, jnp.clip(partner, 0, count - 1), valid


def swap_pairs(swap, count):
    reach, looks = REACH[swap]
    pairs = []
    for low in range(count - reach):
        if (low // reach) % 2 == looks:
            pairs += [(low, low + reach), (low + reach, low)]
    return pairs


def swap_direct(sends):
    count = lax.axis_size("sub")
    return [lax.ppermute(send, "sub", swap_pairs(m, count)) for send, m in zip(sends, DIRECT)]


def swap_all(sends):
    count = lax.axis_size("sub")
    here = lax.axis_index("sub")
    even = lax.rem(here + here // 2, 2) == 0
    far, near, beside = [lax.ppermute(send, "sub", swap_pairs(m, count)) for send, m in zip(sends, (0, 1, 3))]
    half = near.shape[0] // 2
    passed = jnp.where(even, near[half:], far[half:])
    return [far, near, lax.ppermute(passed, "sub", swap_pairs(3, count)), beside]


class Table:
    def __init__(self, faces):
        slots = SWAPS * CAP
        self.own_face, self.far_block, self.far_sign = 0, slots, 2 * slots
        self.slot, self.sign, self.offset = 3 * slots, 3 * slots + faces, 3 * slots + 2 * faces
        self.here = 3 * slots + 3 * faces
        self.which = self.here + 2
        self.spare = self.which + SWAPS
        self.size = -(-(self.spare + 1) // 128) * 128


def rows_of(index, rows=FACE_ROWS):
    return pl.ds(pl.multiple_of(index * rows, rows), rows)


def places(sends, span):
    for send, held in zip(sends, SENDS):
        for k, m in enumerate(held):
            yield send, k * span, m


def pack(sends, source, tab, base):
    for send, at, m in places(sends, CAP * FACE_ROWS):
        for j in range(CAP):
            send[at + j * FACE_ROWS:at + (j + 1) * FACE_ROWS, :] = source[rows_of(tab[base + m * CAP + j]), :]


def copies(pairs, sems):
    made = [pltpu.make_async_copy(source, target, sems.at[i]) for i, (source, target) in enumerate(pairs)]
    for copy in made:
        copy.start()
    return made


def build_table(faces, tab, pos, offs, blks, sgns):
    t = Table(faces)
    count = offs.shape[0]
    here = pos[0]
    tab[t.here] = here
    tab[t.here + 1] = pos[1]
    for i in range(3 * SWAPS * CAP):
        tab[i] = 0
    swaps = [partner_of(m, here, count) for m in range(SWAPS)]
    for m, (which, far, valid) in enumerate(swaps):
        tab[t.which + m] = which
        theirs = jnp.int32(0)
        for f in range(faces):
            hit = valid & (offs[far, f] == 3 - which)
            slot = m * CAP + theirs
            tab[jnp.where(hit, t.far_block + slot, t.spare)] = blks[far, f]
            tab[jnp.where(hit, t.far_sign + slot, t.spare)] = 2 * sgns[far, f] - 1
            theirs = theirs + hit.astype(jnp.int32)
    nexts = [jnp.int32(m * CAP) for m in range(SWAPS)]
    for f in range(faces):
        offset = offs[here, f]
        hits = [offset == which for which, _, _ in swaps]
        slot = sum(jnp.where(hit, value, 0) for hit, value in zip(hits, nexts))
        nexts = [value + hit.astype(jnp.int32) for hit, value in zip(hits, nexts)]
        tab[t.own_face + slot] = f
        tab[t.slot + f] = slot
        tab[t.sign + f] = 2 * sgns[here, f] - 1
        tab[t.offset + f] = offset


def widen_slab(slab, groups):
    rows, columns = slab.shape
    modes_n = rows // groups
    blocks = -(-(columns // modes_n * PAD) // HALF)
    source = lax.broadcasted_iota(jnp.int32, (columns, blocks * 128), 0)
    target = lax.broadcasted_iota(jnp.int32, (columns, blocks * 128), 1)
    place = lax.div(source, modes_n) * PAD + lax.rem(source, modes_n)
    place = lax.div(place, HALF) * 128 + lax.rem(place, HALF)
    target_row = lax.broadcasted_iota(jnp.int32, (PAD * groups, rows), 0)
    source_row = lax.broadcasted_iota(jnp.int32, (PAD * groups, rows), 1)
    deepen = (target_row == lax.div(source_row, modes_n) * PAD + lax.rem(source_row, modes_n)).astype(BF16)
    exact = functools.partial(jnp.dot, preferred_element_type=F32)
    high, low = split(slab[...])
    wide = exact(high, (target == place).astype(BF16)) + exact(low, (target == place + HALF).astype(BF16))
    return exact(deepen, wide.astype(BF16)).astype(BF16)


def start_kernel(faces, steps, groups, pos, offs_h, blks_h, sgns_h, lam_h, modes_h, contact_h, slab_h,
                 tab, rows_out, own_t, own_slab, *rest):
    sends, (wide, side, lam, modes, contact, slab, offs, blks, sgns, sems) = rest[:SWAPS], rest[SWAPS:]
    t = Table(faces)
    made = copies(
        ((offs_h, offs), (blks_h, blks), (sgns_h, sgns), (modes_h, modes), (contact_h, contact), (lam_h, lam),
         (slab_h, slab)), sems)
    wide[...] = jnp.zeros_like(wide)
    for copy in made:
        copy.wait()
    build_table(faces, tab, pos, offs, blks, sgns)
    own_slab[...] = widen_slab(slab, groups)

    modes_n = modes.shape[0]
    high, low = split(modes[...])
    high, low = high.astype(F32), low.astype(F32)
    wide[0:modes_n, :] = high
    wide[PAD:PAD + modes_n, :] = low
    rows_out[...] = wide[0:2 * PAD, :].astype(BF16)
    wide[PAD:PAD + modes_n, :] = high
    wide[2 * PAD:2 * PAD + modes_n, :] = low
    wide[CONTACT_LANE:CONTACT_LANE + steps, :] = contact[...].astype(F32)
    own_t[...] = wide[...].T.astype(BF16)

    wide[PAD:3 * PAD, :] = jnp.zeros_like(wide[PAD:3 * PAD, :])
    wide[PAD:PAD + modes_n, :] = low
    wide[2 * PAD:2 * PAD + steps, :] = contact[...].astype(F32)
    wide[CONTACT_LANE:CONTACT_LANE + steps, :] = jnp.zeros_like(contact, F32)
    side[...] = wide[...].T
    block = CAP * FACE_ROWS
    for send, m in zip(sends, DIRECT):
        beside = jnp.zeros((FACE_ROWS, side.shape[1]), F32)
        for j in range(CAP):
            where = rows_of(tab[t.far_block + m * CAP + j])
            lam_high, lam_low = split(lam[where, :])
            here = j * FACE_ROWS
            send[here:here + FACE_ROWS, :] = lam_high
            send[block + here:block + here + FACE_ROWS, :] = lam_low
            beside = beside + (pltpu.roll(side[where, :], SIDE * j, 1) if j else side[where, :])
        send[2 * block:FIRST_ROWS, :] = beside.astype(BF16)
        for k in range(own_slab.shape[1] // 128):
            here = FIRST_ROWS + k * own_slab.shape[0]
            send[here:here + own_slab.shape[0], :] = own_slab[:, k * 128:(k + 1) * 128]


def spread_out(value, out, counts):
    n_sub, n_grp = counts

    def body(i, carry):
        out[pl.ds(i * n_grp, n_grp)] = value
        return carry

    lax.fori_loop(0, n_sub, body, 0, unroll=n_sub <= 8)


def bands(faces, order):
    rows = faces * FACE_ROWS
    return [slice(at, at + rows) for at in range(0, order, rows)]


def fetch(dual_h, inner, sems, faces):
    face_rows = faces * FACE_ROWS
    rest = bands(faces, dual_h.shape[1])[1:]
    return copies([(dual_h.at[0, band], inner.at[band.start - face_rows:band.stop - face_rows]) for band in rest], sems)


def apply(made, dual, inner, zfull, faces):
    field = zfull[...]
    face_rows = faces * FACE_ROWS
    for copy in made:
        copy.wait()
    for band in bands(faces, zfull.shape[0]):
        rows = dual[...] if band.start == 0 else inner[band.start - face_rows:band.stop - face_rows, :]
        yield band, jnp.dot(rows, field, preferred_element_type=F32).astype(BF16)


def gather(field, zfull, tab, faces):
    t = Table(faces)
    order = zfull.shape[0]
    face_rows = faces * FACE_ROWS
    for f in range(faces):
        own = field[f * FACE_ROWS:(f + 1) * FACE_ROWS, :].astype(BF16).astype(F32)
        far = field[order + f * FACE_ROWS:order + (f + 1) * FACE_ROWS, :].astype(BF16).astype(F32)
        zfull[f * FACE_ROWS:(f + 1) * FACE_ROWS, :] = (own + tab[t.sign + f].astype(F32) * far).astype(BF16)
    zfull[face_rows:, :] = field[face_rows:order, :].astype(BF16)


def first_kernel(faces, groups, tab_v, lam_h, own_t, own_slab, dual_h, loads_h, *rest):
    recvs, (lam_all, all_t, zfull, image, dual, loads, choice), rest = rest[:SWAPS], rest[SWAPS:SWAPS + 7], rest[SWAPS + 7:]
    sends, rest = rest[:len(SENDS)], rest[len(SENDS):]
    pieces, (joined, slabs, picked, tab, sems) = rest[:groups], rest[groups:]
    t = Table(faces)
    order, columns = lam_h.shape
    block = CAP * FACE_ROWS
    face_rows = faces * FACE_ROWS
    made = copies(
        ((tab_v, tab), (lam_h, lam_all.at[0:order]), (dual_h.at[0, 0:face_rows], dual), (loads_h.at[0:face_rows], loads)), sems)
    for m, recv in zip(DIRECT, recvs):
        joined[m * FIRST_ROWS:(m + 1) * FIRST_ROWS, :] = recv[0:FIRST_ROWS, :]
    all_t[0:order, :] = own_t[...]
    made[0].wait()
    lanes = all_t.shape[1]
    lane = lax.broadcasted_iota(jnp.int32, (FACE_ROWS, lanes), 1)
    for f in range(faces):
        slot = tab[t.slot + f]
        turn = lax.rem(slot, CAP)
        start = lax.div(slot, CAP) * (2 * CAP + 1)
        high = joined[rows_of(start + turn), :].astype(F32)
        low = joined[rows_of(start + CAP + turn), :].astype(F32)
        at = order + f * FACE_ROWS
        lam_all[at:at + FACE_ROWS, :] = high + low
        side = joined[rows_of(start + 2 * CAP), :].astype(F32)
        mine = side
        for j in range(1, CAP):
            mine = jnp.where(turn == j, pltpu.roll(side, lanes - SIDE * j, 1), mine)
        high = jnp.where(lane < PAD, mine, 0.0)
        low = jnp.where((lane >= PAD) & (lane < 2 * PAD), mine, 0.0)
        flags = jnp.where((lane >= 2 * PAD) & (lane < 3 * PAD), mine, 0.0)
        trio = high + pltpu.roll(high, PAD, 1) + pltpu.roll(low, PAD, 1)
        placed = pltpu.roll(flags, CONTACT_LANE - 2 * PAD, 1)
        for i in range(len(OFFSETS)):
            moved = pltpu.roll(trio, GROUP * (1 + i), 1)
            placed = placed + jnp.where(tab[t.offset + f] == i, moved, 0.0)
        all_t[at:at + FACE_ROWS, :] = placed.astype(BF16)
    height, width = own_slab.shape
    slabs[0] = own_slab[...].astype(F32)
    for m, recv in zip(DIRECT, recvs):
        parts_in = [recv[FIRST_ROWS + k * height:FIRST_ROWS + (k + 1) * height, :] for k in range(width // 128)]
        slabs[1 + tab[t.which + m]] = jnp.concatenate(parts_in, axis=1).astype(F32)
    for i, piece in enumerate(pieces):
        group = lax.rem(tab[t.here + 1] + i, groups)
        picked[...] = jnp.zeros_like(picked)
        for k in range(len(NEAR)):
            picked[k * PAD:(k + 1) * PAD, :] = slabs[k, pl.ds(pl.multiple_of(group * PAD, PAD), PAD), :]
        piece[...] = picked[...].astype(BF16)
    slot = lax.broadcasted_iota(jnp.int32, choice.shape, 1)
    line = lax.broadcasted_iota(jnp.int32, choice.shape, 0)
    inside = lax.rem(slot, FACE_ROWS)
    chosen = jnp.zeros(choice.shape, jnp.int32)
    for q in range(SWAPS * CAP):
        values = jnp.where(line == 0, tab[t.far_block + q] * FACE_ROWS + inside, tab[t.far_sign + q])
        chosen = jnp.where(lax.div(slot, FACE_ROWS) == q, values, chosen)
    choice[...] = chosen.astype(F32)
    made[1].wait()
    gather(lam_all, zfull, tab, faces)
    made[2].wait()
    image[...] = jnp.dot(dual[...], zfull[...], preferred_element_type=F32).astype(BF16)
    pack(sends, image, tab, t.own_face)
    made[3].wait()


def step_length(parts):
    sums = jnp.sum(parts[...], axis=0)
    return sums[0:1, :] / sums[1:2, :]


def stepped(alpha, lam, dirn, all_t, step, rows):
    value = lam[rows, :] - alpha * dirn[rows, :]
    lane = CONTACT_LANE + step
    active = all_t[rows, lane:lane + 1].astype(F32)
    return jnp.where(active > 0.5, jnp.maximum(value, 0.0), value)


def update_kernel(faces, step, tab_v, dual, parts, lam_all, dirn_all, all_t, lam_next, zfull, image, *rest):
    sends, (tab, sems) = rest[:len(SENDS)], rest[len(SENDS):]
    (enter,) = copies(((tab_v, tab),), sems)
    lam_next[...] = stepped(step_length(parts), lam_all, dirn_all, all_t, step, slice(0, lam_all.shape[0]))
    enter.wait()
    gather(lam_next, zfull, tab, faces)
    image[...] = jnp.dot(dual[...], zfull[...], preferred_element_type=F32).astype(BF16)
    pack(sends, image, tab, Table(faces).own_face)


def residual_of(rows, grad):
    high, low = split(grad)
    columns = grad.shape[1]
    prod = jnp.dot(rows, jnp.concatenate([high, low], axis=1), preferred_element_type=F32)
    return prod[0:PAD, 0:columns] + (prod[PAD:2 * PAD, 0:columns] + prod[0:PAD, columns:2 * columns])


def inner_kernel(faces, dual_h, loads_h, zfull, rows, grad, residual, dual, loads, sems):
    order = zfull.shape[0]
    inner = bands(faces, order)[1:]
    face_rows = faces * FACE_ROWS
    made = fetch(dual_h, dual, sems, faces)
    (enter,) = copies(((loads_h.at[face_rows:order], loads),), sems.at[len(made):])
    field = zfull[...]
    enter.wait()
    for copy, band in zip(made, inner):
        copy.wait()
        here = slice(band.start - face_rows, band.stop - face_rows)
        image = jnp.dot(dual[here, :], field, preferred_element_type=F32).astype(BF16)
        grad[here, :] = image.astype(F32) - loads[here, :]
    residual[...] = residual_of(rows[:, face_rows:], grad[...])


def last_kernel(faces, step, parts, lam, dirn, all_t, out_h, out, sems):
    alpha = step_length(parts)
    made = []
    for i, band in enumerate(bands(faces, out.shape[0])):
        out[band, :] = stepped(alpha, lam, dirn, all_t, step, band)
        made += copies([(out.at[band], out_h.at[band])], sems.at[i:])
    for copy in made:
        copy.wait()


def spread_kernel(faces, first, counts, tab_v, choice, image, loads, rows, part, *rest):
    if first:
        pieces, rest = rest[:counts[1]], rest[counts[1]:]
    recvs, (grad, pay_h), rest = rest[:SWAPS], rest[SWAPS:SWAPS + 2], rest[SWAPS + 2:]
    sends, rest = rest[:len(SENDS)], rest[len(SENDS):]
    if first:
        inverse, rest = rest[0], rest[1:]
    if first:
        sorted_, rest = rest[0], rest[1:]
    low_grad, pay, tab, sems = rest
    (enter,) = copies(((tab_v, tab),), sems)
    t = Table(faces)
    n_sub, n_grp = counts
    face_rows = faces * FACE_ROWS
    columns = loads.shape[1]
    line = lax.broadcasted_iota(jnp.int32, (face_rows, choice.shape[1]), 0).astype(F32)
    select = jnp.where(line == choice[0:1, :], choice[1:2, :], 0.0).astype(BF16)
    came = jnp.concatenate([recv[0:CAP * FACE_ROWS, :] for recv in recvs], axis=0)
    returned = jnp.dot(select, came, preferred_element_type=F32)
    grad[...] = image[...].astype(F32) - loads[...] + returned
    low_grad[...] = grad[...].astype(BF16)
    residual = part[...] + residual_of(rows[:, 0:face_rows], grad[...])

    spread_out(jnp.broadcast_to(residual[None], (n_grp,) + residual.shape), pay, counts)
    (leave,) = copies(((pay, pay_h),), sems.at[1:])
    enter.wait()
    pack(sends, low_grad, tab, t.far_block)
    if first:
        inverse[...] = inverse_rows(pieces, tab[t.here + 1], sorted_)
    leave.wait()


def inverse_rows(pieces, group, ordered):
    groups = len(pieces)
    for i, piece in enumerate(pieces):
        ordered[lax.rem(group + groups - i, groups)] = piece[...].astype(F32)
    width = ordered.shape[2]
    blocks = [ordered[g, :, k:k + 128] for g in range(groups) for k in range(0, width, 128)]
    lane = lax.broadcasted_iota(jnp.int32, blocks[0].shape, 1)
    pairs = list(zip(blocks[0::2], blocks[1::2]))
    high = [jnp.where(lane < HALF, one, pltpu.roll(two, HALF, 1)) for one, two in pairs]
    low = [jnp.where(lane < HALF, pltpu.roll(one, HALF, 1), two) for one, two in pairs]
    return jnp.concatenate(high + high + low, axis=1).astype(BF16)


def direction_kernel(faces, tab_v, dual_h, dual, near, grad, grad_in, every, all_t, *rest):
    (far, passed, beside), rest = rest[:SWAPS - 1], rest[SWAPS - 1:]
    recvs = far, near, passed, beside
    (inverse, dirn, parts), rest = rest[:3], rest[3:]
    zfull, joined, grad_all, moved, tab, sems = rest
    (enter,) = copies(((tab_v, tab),), sems)
    made = fetch(dual_h, moved, sems.at[1:], faces)
    t = Table(faces)
    columns = grad.shape[1]
    order = grad.shape[0] + grad_in.shape[0]
    face_rows = faces * FACE_ROWS
    block = CAP * FACE_ROWS
    for m, recv in enumerate(recvs):
        joined[m * block:(m + 1) * block, :] = recv[0:block, :]
    enter.wait()
    for f in range(faces):
        at = f * FACE_ROWS
        grad_all[at:at + FACE_ROWS, :] = joined[rows_of(tab[t.slot + f]), :].astype(F32)
    residual = every[...].reshape(every.shape[0] * PAD, columns)
    high, low = split(residual)
    stacked = jnp.concatenate([high, low, high], axis=0)
    corr = jnp.dot(inverse[...], stacked, preferred_element_type=F32)
    pieces = []
    for k in range(len(NEAR)):
        high, low = split(corr[k * PAD:(k + 1) * PAD, :])
        pieces += [high.astype(F32), low.astype(F32), high.astype(F32)]
    pieces.append(jnp.zeros((all_t.shape[1] - CONTACT_LANE, columns), F32))
    weights = jnp.concatenate(pieces, axis=0).astype(BF16)
    shift = jnp.dot(all_t[...], weights, preferred_element_type=F32)
    dirn[order:, :] = grad_all[...] - shift[order:, :]
    dirn[0:face_rows, :] = grad[...] - shift[0:face_rows, :]
    dirn[face_rows:order, :] = grad_in[...] - shift[face_rows:order, :]
    gather(dirn, zfull, tab, faces)
    curv = jnp.zeros((1, columns), F32)
    for band, product in apply(made, dual, moved, zfull, faces):
        image = product.astype(F32)
        if band.start > 0:
            curv = curv + jnp.sum(dirn[band, :] * image, axis=0, keepdims=True)
            continue
        for f in range(faces):
            at = f * FACE_ROWS
            far = dirn[order + at:order + at + FACE_ROWS, :]
            gathered = dirn[at:at + FACE_ROWS, :] + tab[t.sign + f].astype(F32) * far
            curv = curv + jnp.sum(gathered * image[at:at + FACE_ROWS, :], axis=0, keepdims=True)
    slope = jnp.sum(grad[...] * dirn[0:face_rows, :], axis=0, keepdims=True)
    slope = slope + jnp.sum(grad_in[...] * dirn[face_rows:order, :], axis=0, keepdims=True)
    both = jnp.concatenate([slope, curv], axis=0)
    parts[...] = jnp.broadcast_to(both[None], parts.shape)


SMEM = pltpu.SMEM
VMEM = pltpu.VMEM
HBM = pltpu.HBM


def call(kernel, name, args, outs, scratch=(), scalars=(), copying=0, cost=None):
    size = 0
    held = [(a.shape, a.dtype) for a, space in args if space == VMEM] + [o[:2] for o in outs if o[2] == VMEM]
    for shape, dtype in held + list(scratch):
        shape = (1,) * (2 - len(shape)) + tuple(shape)
        padded = shape[:-2] + (-(-shape[-2] // 16) * 16, -(-shape[-1] // 128) * 128)
        count = jnp.dtype(dtype).itemsize
        for length in padded:
            count *= length
        size += count
    return pl.pallas_call(
        kernel,
        name=name,
        out_shape=[(HBM if space == HBM else jax.ShapeDtypeStruct)(shape, dtype) for shape, dtype, space in outs],
        in_specs=[pl.BlockSpec(memory_space=space) for _, space in args],
        out_specs=[pl.BlockSpec(memory_space=space) for _, _, space in outs],
        scratch_shapes=[pltpu.VMEM(shape, dtype) for shape, dtype in scratch]
        + [pltpu.SMEM(shape, dtype) for shape, dtype in scalars]
        + ([pltpu.SemaphoreType.DMA((copying,))] if copying else []),
        compiler_params=pltpu.CompilerParams(vmem_limit_bytes=size + (6 << 20)),
        cost_estimate=cost,
    )(*[a for a, _ in args])


def vmem(*arrays):
    return [(a, VMEM) for a in arrays]


def hbm(*arrays):
    return [(pltpu.with_memory_space_constraint(a, HBM), HBM) for a in arrays]


def turn(value, ahead):
    count = lax.axis_size("grp")
    return lax.ppermute(value, "grp", [(g, (g + ahead) % count) for g in range(count)])


def exchange(value):
    return lax.all_to_all(value, ("sub", "grp"), 0, 0)


def on_device(
    lam_start, loads, dual_ops, modes, coarse_inverse, face_offset, face_block, face_sign, contact
):
    n_sub, n_grp = lax.axis_size("sub"), lax.axis_size("grp")
    counts = (n_sub, n_grp)
    everyone = n_sub * n_grp
    order, columns = lam_start.shape
    faces = face_offset.shape[-1]
    steps = contact.shape[0]
    halo = faces * FACE_ROWS
    block = CAP * FACE_ROWS
    t = Table(faces)
    modes_n = coarse_inverse.shape[0] // n_grp
    blocks = -(-(coarse_inverse.shape[1] // modes_n * PAD) // HALF)
    slab_shape = (PAD * n_grp, blocks * 128)
    piece = (COARSE, blocks * 128)
    pos = jnp.stack([lax.axis_index("sub"), lax.axis_index("grp")]).astype(jnp.int32)
    flat = hbm(*[a.reshape(n_sub, faces) for a in (face_offset, face_block, face_sign)])
    sent = [((len(held) * block, columns), BF16, VMEM) for held in SENDS]

    tab, rows, own_t, own_slab, *sends = call(
        functools.partial(start_kernel, faces, steps, n_grp), "start",
        [(pos, SMEM)] + flat + hbm(lam_start, modes, contact, coarse_inverse),
        [((t.size,), jnp.int32, SMEM), ((2 * PAD, order), BF16, VMEM), ((order, 128), BF16, VMEM),
         (slab_shape, BF16, VMEM)]
        + [((FIRST_ROWS + slab_shape[0] * slab_shape[1] // 128, columns), BF16, VMEM)] * SWAPS,
        [((128, order), F32), ((order, 128), F32), (lam_start.shape, F32), (modes.shape, F32), (contact.shape, jnp.int32),
         (coarse_inverse.shape, F32)],
        [((n_sub, faces), jnp.int32)] * 3, 7,
    )
    recvs = swap_direct(sends)
    table = [((t.size,), jnp.int32)]
    matrix = ((order - halo, order), BF16)
    parts_n = order // halo
    lam_all, all_t, zfull, image, dual, face_loads, choice, *sends = call(
        functools.partial(first_kernel, faces, n_grp), "first",
        vmem(tab) + hbm(lam_start) + vmem(own_t, own_slab) + hbm(dual_ops, loads) + vmem(*recvs),
        [((order + halo, columns), F32, VMEM), ((order + halo, 128), BF16, VMEM), ((order, columns), BF16, VMEM),
         ((halo, columns), BF16, VMEM), ((halo, order), BF16, VMEM),
         ((halo, columns), F32, VMEM), ((8, SWAPS * block), F32, VMEM)] + sent
        + [(piece, BF16, VMEM)] * n_grp,
        [((SWAPS * FIRST_ROWS, columns), BF16), ((len(NEAR),) + slab_shape, F32), (piece, F32)], table, 4,
    )
    sends, pieces = sends[:len(SENDS)], sends[len(SENDS):]
    for step in range(steps):
        first = step == 0
        returned = swap_all(sends)
        grad_in, part = call(
            functools.partial(inner_kernel, faces), "inner",
            hbm(dual_ops, loads) + vmem(zfull, rows),
            [((order - halo, columns), F32, VMEM), ((PAD, columns), F32, VMEM)],
            [((order - halo, order), BF16), ((order - halo, columns), F32)], (), parts_n,
            pl.CostEstimate(flops=2 * (order - halo) * order * columns, transcendentals=0,
                            bytes_accessed=2 * (order - halo) * order),
        )
        if first:
            pieces = [pieces[0]] + [turn(value, i) for i, value in enumerate(pieces) if i]
        made = [((COARSE, 3 * PAD * everyone), BF16, VMEM)]
        grad, pay, *sends = call(
            functools.partial(spread_kernel, faces, first, counts), "spread",
            vmem(tab, choice, image, face_loads, rows, part, *(pieces if first else []), *returned),
            [((halo, columns), F32, VMEM), ((everyone, PAD, columns), F32, HBM)] + sent + (made if first else []),
            ([((n_grp,) + piece, F32)] if first else []) + [((halo, columns), BF16), ((everyone, PAD, columns), F32)], table, 2,
        )
        if first:
            inverse = sends.pop()
        far, near, passed, beside = swap_all(sends)
        every = exchange(pay)
        dirn, parts = call(
            functools.partial(direction_kernel, faces), "direction",
            vmem(tab) + hbm(dual_ops) + vmem(dual, near, grad, grad_in, every, all_t, far, passed, beside, inverse),
            [((order + halo, columns), F32, VMEM), ((everyone, 2, columns), F32, VMEM)],
            [((order, columns), BF16), ((SWAPS * block, columns), BF16), ((halo, columns), F32), matrix], table, parts_n,
        )
        parts = exchange(parts)
        if step < steps - 1:
            lam_all, zfull, image, *sends = call(
                functools.partial(update_kernel, faces, step), "update",
                vmem(tab, dual, parts, lam_all, dirn, all_t),
                [((order + halo, columns), F32, VMEM), ((order, columns), BF16, VMEM), ((halo, columns), BF16, VMEM)] + sent,
                [], table, 1,
            )
    return call(
        functools.partial(last_kernel, faces, steps - 1), "last",
        vmem(parts, lam_all, dirn, all_t),
        [((order, columns), F32, HBM)], [((order, columns), F32)], (), order // halo,
    )[0]


def solution(mesh):
    return jax.shard_map(
        on_device,
        mesh=mesh,
        in_specs=(
            P(("sub", "grp"), None),
            P(("sub", "grp"), None),
            P(("sub", "grp"), None, None),
            P(None, ("sub", "grp")),
            P("sub", "grp"),
            P(None, "grp", None),
            P(None, "grp", None),
            P(None, "grp", None),
            P(None, ("sub", "grp")),
        ),
        out_specs=P(("sub", "grp"), None),
        check_vma=False,
    )
```

time: 571 us -> 135 us (0.24)
  blocking collectives: 260 us -> 27.9 us
  starting transfers between devices: 136 us -> 54.3 us
  matrix products: 80.8 us -> 0 us
  local copies, waits for them, and re-layouts: 56.6 us -> 0 us
  Pallas kernels: 0 us -> 24.6 us
  other arithmetic: 21 us -> 0.12 us
  waiting for transfers between devices: 10.3 us -> 27 us
    all_gather x4 -> x0, blocking collectives: 131 us -> none  [the longest x3 125 us: coarse_direction(): every_res = lax.all_gather(residual, ('sub', 'grp'), axis=0, tiled=True)]
    psum x3 -> x0, blocking collectives: 130 us -> none  [on_device(): slope = lax.psum(local_slope, ('sub', 'grp'))]
    ppermute x48 -> x31, starting transfers between devices: 136 us -> 44.8 us  [the longest x18 30.7 us: swap_all(): lax.ppermute(send, 'sub', swap_pairs(m, count))]
    dot_general x119 -> x0, matrix products: 80.8 us -> none  [the longest x24 16.3 us: apply_dual(): jnp.einsum('jb,brl->jrl', pack, faces, preferred_element_type=jnp.float32)]
    all_to_all x0 -> x3, blocking collectives: none -> 27.9 us  [exchange(): return lax.all_to_all(value, ('sub', 'grp'), 0, 0)]
    slice x35 -> x0, local copies, waits for them, and re-layouts: 25.4 us -> none  [the longest x12 6.91 us: apply_dual(): yfaces = image[:face_total].reshape(FACES, FACE_ROWS, normal_loads)]
    pallas_call x0 -> x14, Pallas kernels: none -> 24.6 us  [call(): pl.pallas_call(kernel, name=name, out_shape=[(HBM if space == HBM else ja...]
    unnamed x118 -> x0, local copies, waits for them, and re-layouts: 13.8 us -> none
  transfers between devices with their start and end apart: 48 -> 34, of which waited for: 11 -> 15; matrix products, arithmetic and copies ran while one was open for 8% -> 0% of each run, Pallas kernels for 0% -> 6%
where the time goes in v1:
time: 135 us; the launch traced here: 134 us
  starting transfers between devices  54.3 us (40%)
  blocking collectives  27.9 us (21%)
  waiting for transfers between devices  27 us (20%)
  Pallas kernels  24.6 us (18%)
    ppermute x18, starting transfers between devices, swap_all(): lax.ppermute(send, 'sub', swap_pairs(m, count))  30.7 us
    all_to_all x3, blocking collectives, exchange(): return lax.all_to_all(value, ('sub', 'grp'), 0, 0)  27.9 us
    pallas_call x14, Pallas kernels, call(): pl.pallas_call(kernel, name=name, out_shape=[(HBM if space == HBM else ja...  24.6 us
    ppermute x18, waiting for transfers between devices, swap_all(): lax.ppermute(send, 'sub', swap_pairs(m, count))  9.96 us
    all_to_all x3, starting transfers between devices, exchange(): return lax.all_to_all(value, ('sub', 'grp'), 0, 0)  9.48 us
    ppermute x4, starting transfers between devices, swap_direct(): lax.ppermute(send, 'sub', swap_pairs(m, count))  7.25 us
    ppermute x6, waiting for transfers between devices, swap_all(): lax.ppermute(passed, 'sub', swap_pairs(3, count))  7.06 us
    all_to_all x3, waiting for transfers between devices, exchange(): return lax.all_to_all(value, ('sub', 'grp'), 0, 0)  6.83 us
  transfers between devices with their start and end apart: 34, of which 15 were waited for; matrix products, arithmetic and copies ran while one was open for 0% of the time, Pallas kernels for 6%

profile of v1, /device:TPU:0, one launch (start us, length us, event | category | flops | bytes accessed | tf_op | source)
XLA Modules:
  0.0 134.2 jit_solution(1824618142955133555)
XLA Ops:
  0.1 2.8 %start.1 = (s32[128]{0:T(128)S(1)}, bf16[16,1024]{1,0:T(8,128)(2,1)S(1)}, bf16[1024,128]{1,0:T(8,128)(2,1)S(1)}, bf16[32,128]{1,0:T(8,128)(2,1)S(1)}, bf16[320,1...) custom-call(s32[2]{0:T(128)S(1)} %pad_add_fusion.pos, ...), custom_call_target="tpu_custom_call" | custom-call | tf_op jit(solution)/shard_map/start/pallas_call | solution.py:465
  2.9 3.1 %collective-permute-start = (bf16[320,128]{1,0:T(8,128)(2,1)S(1)}, bf16[320,128]{1,0:T(8,128)(2,1)S(1)}, u32[]{:S(2)}, u32[]{:S(2)}) collective-permute-start(bf16[320,128]{1,0:T(8,128)(2,1)S(1)} %get-tuple-element.70), channel_id=1, source_target_pairs={{0,8},{8,0},{4,12},{12,4},{16,24},{24,16},{20,28},{28,20},{1,9},{9... | collective-permute-start | bytes 245768 | tf_op jit(solution)/shard_map/ppermute | solution.py:55
  7.3 2.8 %collective-permute-start.3 = (bf16[320,128]{1,0:T(8,128)(2,1)S(1)}, bf16[320,128]{1,0:T(8,128)(2,1)S(1)}, u32[]{:S(2)}, u32[]{:S(2)}) collective-permute-start(bf16[320,128]{1,0:T(8,128)(2,1)S(1)} %get-tuple-element.73), channel_id=1, source_target_pairs={{0,4},{4,0},{8,12},{12,8},{16,20},{20,16},{24,28},{28,24},{1,5},{5... | collective-permute-start | bytes 245768 | tf_op jit(solution)/shard_map/ppermute | solution.py:55
  10.1 3.2 %collective-permute-done.3.rest_3_ = bf16[320,128]{1,0:T(8,128)(2,1)S(1)} collective-permute-done((bf16[320,128]{1,0:T(8,128)(2,1)S(1)}, bf16[320,128]{1,0:T(8,128)(2,1)S(1)}, u32[]{:S(2)}, u32[]{:S(2)}) %collective-permute-start.3) | collective-permute-done | bytes 81952 | tf_op jit(solution)/shard_map/ppermute | solution.py:55
  15.5 7.3 %collective-permute-start.8 = (bf16[256,128]{1,0:T(8,128)(2,1)S(1)}, bf16[256,128]{1,0:T(8,128)(2,1)S(1)}, u32[]{:S(2)}, u32[]{:S(2)}) collective-permute-start(bf16[256,128]{1,0:T(8,128)(2,1)S(1)} %get-tuple-element.86), channel_id=1, source_target_pairs={{0,8},{8,0},{4,12},{12,4},{16,24},{24,16},{20,28},{28,20},{1,9},{9... | collective-permute-start | bytes 196616 | tf_op jit(solution)/shard_map/ppermute | solution.py:62
  29.7 2.5 %inner.3 = (f32[768,128]{1,0:T(8,128)S(1)}, f32[8,128]{1,0:T(8,128)S(1)}) custom-call(bf16[1,1024,1024]{2,1,0:T(8,128)(2,1)} %dual_h.13, f32[1024,128]{1,0:T(8,128)} %loads_h.7, bf16[1024,128]{1,0:T(8,128)(2,1)S(1)} %get-tuple-element.79.zfull, bf16[16,1024]{1,0:T(8,128)(2,1)S(1)} %get-tuple-element.78.rows), custom_call_target="tpu_custom_call" | custom-call | flops 201326592 | bytes 1572864 | tf_op jit(solution)/shard_map/inner/pallas_call | solution.py:465
  33.3 2.1 %collective-permute-start.11 = (bf16[256,128]{1,0:T(8,128)(2,1)S(1)}, bf16[256,128]{1,0:T(8,128)(2,1)S(1)}, u32[]{:S(2)}, u32[]{:S(2)}) collective-permute-start(bf16[256,128]{1,0:T(8,128)(2,1)S(1)} %get-tuple-element.88), channel_id=1, source_target_pairs={{0,8},{8,0},{4,12},{12,4},{16,24},{24,16},{20,28},{28,20},{1,9},{9... | collective-permute-start | bytes 196616 | tf_op jit(solution)/shard_map/ppermute | solution.py:62
  36.1 3.1 %all-to-all-start = ((f32[32,8,128]{2,1,0:T(8,128)}), f32[32,8,128]{2,1,0:T(8,128)S(1)}, u32[]{:S(2)}, u32[]{:S(2)}) async-start(f32[32,8,128]{2,1,0:T(8,128)} %get-tuple-element.91), calls=%async_computation | async-start | bytes 262144 | tf_op jit(solution)/shard_map/all_to_all | solution.py:493
  39.2 1.8 %collective-permute-start.14 = (bf16[128,128]{1,0:T(8,128)(2,1)S(1)}, bf16[128,128]{1,0:T(8,128)(2,1)S(1)}, u32[]{:S(2)}, u32[]{:S(2)}) collective-permute-start(bf16[128,128]{1,0:T(8,128)(2,1)S(1)} %get-tuple-element.94), channel_id=1, source_target_pairs={{0,4},{4,0},{8,12},{12,8},{16,20},{20,16},{24,28},{28,24},{1,5},{5... | collective-permute-start | bytes 98312 | tf_op jit(solution)/shard_map/ppermute | solution.py:62
  41.4 2.0 %collective-permute-done.14.rest_2_ = bf16[128,128]{1,0:T(8,128)(2,1)S(1)} collective-permute-done((bf16[128,128]{1,0:T(8,128)(2,1)S(1)}, bf16[128,128]{1,0:T(8,128)(2,1)S(1)}, u32[]{:S(2)}, u32[]{:S(2)}) %collective-permute-start.14) | collective-permute-done | bytes 32800 | tf_op jit(solution)/shard_map/ppermute | solution.py:62
  45.1 2.3 %all-to-all-done.every = f32[32,8,128]{2,1,0:T(8,128)S(1)} async-done(((f32[32,8,128]{2,1,0:T(8,128)}), f32[32,8,128]{2,1,0:T(8,128)S(1)}, u32[]{:S(2)}, u32[]{:S(2)}) %all-to-all-start) | async-done | bytes 131104 | tf_op jit(solution)/shard_map/all_to_all | solution.py:493
  47.4 2.2 %direction.3 = (f32[1280,128]{1,0:T(8,128)S(1)}, f32[32,2,128]{2,1,0:T(2,128)S(1)}) custom-call(s32[128]{0:T(128)S(1)} %get-tuple-element.67.tab_v, bf16[1,1024,1024]{2,1,0:T(8,128)(2,1)} %dual_h.13, bf16[256,1024]{1,0:T(8,128)(2,1)S(1)} %get-tuple-element.74.dual, bf16[256,128]{1,0:T(8,128)(2,1)S(1)} %collective-permute-done.11.near, ...), custom_call_target="tpu_custom_call" | custom-call | tf_op jit(solution)/shard_map/direction/pallas_call | solution.py:465
  49.6 9.3 %all_to_all.30.parts = f32[32,2,128]{2,1,0:T(2,128)S(1)} all-to-all(f32[32,2,128]{2,1,0:T(2,128)S(1)} %get-tuple-element.96), channel_id=1, replica_groups=mesh['sub'=8,'grp'=4] {'sub','grp'}, dimensions={0} | all-to-all | bytes 65536 | tf_op jit(solution)/shard_map/all_to_all | solution.py:493
  60.7 2.5 %collective-permute-start.16 = (bf16[256,128]{1,0:T(8,128)(2,1)S(1)}, bf16[256,128]{1,0:T(8,128)(2,1)S(1)}, u32[]{:S(2)}, u32[]{:S(2)}) collective-permute-start(bf16[256,128]{1,0:T(8,128)(2,1)S(1)} %get-tuple-element.103), channel_id=1, source_target_pairs={{0,8},{8,0},{4,12},{12,4},{16,24},{24,16},{20,28},{28,20},{1,9},{9... | collective-permute-start | bytes 196616 | tf_op jit(solution)/shard_map/ppermute | solution.py:62
  66.0 2.5 %inner.4 = (f32[768,128]{1,0:T(8,128)S(1)}, f32[8,128]{1,0:T(8,128)S(1)}) custom-call(bf16[1,1024,1024]{2,1,0:T(8,128)(2,1)} %dual_h.13, f32[1024,128]{1,0:T(8,128)} %loads_h.7, bf16[1024,128]{1,0:T(8,128)(2,1)S(1)} %get-tuple-element.100.zfull, bf16[16,1024]{1,0:T(8,128)(2,1)S(1)} %get-tuple-element.78.rows), custom_call_target="tpu_custom_call" | custom-call | flops 201326592 | bytes 1572864 | tf_op jit(solution)/shard_map/inner/pallas_call | solution.py:465
  70.4 2.1 %collective-permute-start.19 = (bf16[256,128]{1,0:T(8,128)(2,1)S(1)}, bf16[256,128]{1,0:T(8,128)(2,1)S(1)}, u32[]{:S(2)}, u32[]{:S(2)}) collective-permute-start(bf16[256,128]{1,0:T(8,128)(2,1)S(1)} %get-tuple-element.105), channel_id=1, source_target_pairs={{0,8},{8,0},{4,12},{12,4},{16,24},{24,16},{20,28},{28,20},{1,9},{9... | collective-permute-start | bytes 196616 | tf_op jit(solution)/shard_map/ppermute | solution.py:62
  73.2 3.2 %all-to-all-start.2 = ((f32[32,8,128]{2,1,0:T(8,128)}), f32[32,8,128]{2,1,0:T(8,128)S(1)}, u32[]{:S(2)}, u32[]{:S(2)}) async-start(f32[32,8,128]{2,1,0:T(8,128)} %get-tuple-element.108), calls=%async_computation.2 | async-start | bytes 262144 | tf_op jit(solution)/shard_map/all_to_all | solution.py:493
  76.4 1.8 %collective-permute-start.22 = (bf16[128,128]{1,0:T(8,128)(2,1)S(1)}, bf16[128,128]{1,0:T(8,128)(2,1)S(1)}, u32[]{:S(2)}, u32[]{:S(2)}) collective-permute-start(bf16[128,128]{1,0:T(8,128)(2,1)S(1)} %get-tuple-element.110), channel_id=1, source_target_pairs={{0,4},{4,0},{8,12},{12,8},{16,20},{20,16},{24,28},{28,24},{1,5},{5... | collective-permute-start | bytes 98312 | tf_op jit(solution)/shard_map/ppermute | solution.py:62
  78.5 2.0 %collective-permute-done.22.rest_2_ = bf16[128,128]{1,0:T(8,128)(2,1)S(1)} collective-permute-done((bf16[128,128]{1,0:T(8,128)(2,1)S(1)}, bf16[128,128]{1,0:T(8,128)(2,1)S(1)}, u32[]{:S(2)}, u32[]{:S(2)}) %collective-permute-start.22) | collective-permute-done | bytes 32800 | tf_op jit(solution)/shard_map/ppermute | solution.py:62
  82.3 2.3 %all-to-all-done.2.every = f32[32,8,128]{2,1,0:T(8,128)S(1)} async-done(((f32[32,8,128]{2,1,0:T(8,128)}), f32[32,8,128]{2,1,0:T(8,128)S(1)}, u32[]{:S(2)}, u32[]{:S(2)}) %all-to-all-start.2) | async-done | bytes 131104 | tf_op jit(solution)/shard_map/all_to_all | solution.py:493
  84.6 2.2 %direction.4 = (f32[1280,128]{1,0:T(8,128)S(1)}, f32[32,2,128]{2,1,0:T(2,128)S(1)}) custom-call(s32[128]{0:T(128)S(1)} %get-tuple-element.67.tab_v, bf16[1,1024,1024]{2,1,0:T(8,128)(2,1)} %dual_h.13, bf16[256,1024]{1,0:T(8,128)(2,1)S(1)} %get-tuple-element.74.dual, bf16[256,128]{1,0:T(8,128)(2,1)S(1)} %collective-permute-done.19.near, ...), custom_call_target="tpu_custom_call" | custom-call | tf_op jit(solution)/shard_map/direction/pallas_call | solution.py:465
  86.8 9.3 %all_to_all.31.parts = f32[32,2,128]{2,1,0:T(2,128)S(1)} all-to-all(f32[32,2,128]{2,1,0:T(2,128)S(1)} %get-tuple-element.111), channel_id=1, replica_groups=mesh['sub'=8,'grp'=4] {'sub','grp'}, dimensions={0} | all-to-all | bytes 65536 | tf_op jit(solution)/shard_map/all_to_all | solution.py:493
  97.8 2.5 %collective-permute-start.24 = (bf16[256,128]{1,0:T(8,128)(2,1)S(1)}, bf16[256,128]{1,0:T(8,128)(2,1)S(1)}, u32[]{:S(2)}, u32[]{:S(2)}) collective-permute-start(bf16[256,128]{1,0:T(8,128)(2,1)S(1)} %get-tuple-element.118), channel_id=1, source_target_pairs={{0,8},{8,0},{4,12},{12,4},{16,24},{24,16},{20,28},{28,20},{1,9},{9... | collective-permute-start | bytes 196616 | tf_op jit(solution)/shard_map/ppermute | solution.py:62
  103.2 2.5 %inner.5 = (f32[768,128]{1,0:T(8,128)S(1)}, f32[8,128]{1,0:T(8,128)S(1)}) custom-call(bf16[1,1024,1024]{2,1,0:T(8,128)(2,1)} %dual_h.13, f32[1024,128]{1,0:T(8,128)} %loads_h.7, bf16[1024,128]{1,0:T(8,128)(2,1)S(1)} %get-tuple-element.115.zfull, bf16[16,1024]{1,0:T(8,128)(2,1)S(1)} %get-tuple-element.78.rows), custom_call_target="tpu_custom_call" | custom-call | flops 201326592 | bytes 1572864 | tf_op jit(solution)/shard_map/inner/pallas_call | solution.py:465
  107.6 2.1 %collective-permute-start.27 = (bf16[256,128]{1,0:T(8,128)(2,1)S(1)}, bf16[256,128]{1,0:T(8,128)(2,1)S(1)}, u32[]{:S(2)}, u32[]{:S(2)}) collective-permute-start(bf16[256,128]{1,0:T(8,128)(2,1)S(1)} %get-tuple-element.120), channel_id=1, source_target_pairs={{0,8},{8,0},{4,12},{12,4},{16,24},{24,16},{20,28},{28,20},{1,9},{9... | collective-permute-start | bytes 196616 | tf_op jit(solution)/shard_map/ppermute | solution.py:62
  110.3 3.2 %all-to-all-start.4 = ((f32[32,8,128]{2,1,0:T(8,128)}), f32[32,8,128]{2,1,0:T(8,128)S(1)}, u32[]{:S(2)}, u32[]{:S(2)}) async-start(f32[32,8,128]{2,1,0:T(8,128)} %get-tuple-element.123), calls=%async_computation.4 | async-start | bytes 262144 | tf_op jit(solution)/shard_map/all_to_all | solution.py:493
  113.5 1.8 %collective-permute-start.30 = (bf16[128,128]{1,0:T(8,128)(2,1)S(1)}, bf16[128,128]{1,0:T(8,128)(2,1)S(1)}, u32[]{:S(2)}, u32[]{:S(2)}) collective-permute-start(bf16[128,128]{1,0:T(8,128)(2,1)S(1)} %get-tuple-element.125), channel_id=1, source_target_pairs={{0,4},{4,0},{8,12},{12,8},{16,20},{20,16},{24,28},{28,24},{1,5},{5... | collective-permute-start | bytes 98312 | tf_op jit(solution)/shard_map/ppermute | solution.py:62
  115.7 2.0 %collective-permute-done.30.rest_2_ = bf16[128,128]{1,0:T(8,128)(2,1)S(1)} collective-permute-done((bf16[128,128]{1,0:T(8,128)(2,1)S(1)}, bf16[128,128]{1,0:T(8,128)(2,1)S(1)}, u32[]{:S(2)}, u32[]{:S(2)}) %collective-permute-start.30) | collective-permute-done | bytes 32800 | tf_op jit(solution)/shard_map/ppermute | solution.py:62
  117.7 1.8 %collective-permute-done.29.rest_1_ = bf16[128,128]{1,0:T(8,128)(2,1)S(1)} collective-permute-done((bf16[128,128]{1,0:T(8,128)(2,1)S(1)}, bf16[128,128]{1,0:T(8,128)(2,1)S(1)}, u32[]{:S(2)}, u32[]{:S(2)}) %collective-permute-start.29) | collective-permute-done | bytes 32800 | tf_op jit(solution)/shard_map/ppermute | solution.py:65
  119.5 2.3 %all-to-all-done.4.every = f32[32,8,128]{2,1,0:T(8,128)S(1)} async-done(((f32[32,8,128]{2,1,0:T(8,128)}), f32[32,8,128]{2,1,0:T(8,128)S(1)}, u32[]{:S(2)}, u32[]{:S(2)}) %all-to-all-start.4) | async-done | bytes 131104 | tf_op jit(solution)/shard_map/all_to_all | solution.py:493
  121.8 2.2 %direction.5 = (f32[1280,128]{1,0:T(8,128)S(1)}, f32[32,2,128]{2,1,0:T(2,128)S(1)}) custom-call(s32[128]{0:T(128)S(1)} %get-tuple-element.67.tab_v, bf16[1,1024,1024]{2,1,0:T(8,128)(2,1)} %dual_h.13, bf16[256,1024]{1,0:T(8,128)(2,1)S(1)} %get-tuple-element.74.dual, bf16[256,128]{1,0:T(8,128)(2,1)S(1)} %collective-permute-done.27.near, ...), custom_call_target="tpu_custom_call" | custom-call | tf_op jit(solution)/shard_map/direction/pallas_call | solution.py:465
  124.0 9.3 %all_to_all.32.parts = f32[32,2,128]{2,1,0:T(2,128)S(1)} all-to-all(f32[32,2,128]{2,1,0:T(2,128)S(1)} %get-tuple-element.126), channel_id=1, replica_groups=mesh['sub'=8,'grp'=4] {'sub','grp'}, dimensions={0} | all-to-all | bytes 65536 | tf_op jit(solution)/shard_map/all_to_all | solution.py:493
  (60 shorter events, 31.9 us)
Async XLA Ops:
  2.9 7.3 %collective-permute-start = (bf16[320,128]{1,0:T(8,128)(2,1)S(1)}, bf16[320,128]{1,0:T(8,128)(2,1)S(1)}, u32[]{:S(2)}, u32[]{:S(2)}) collective-permute-start(bf16[320,128]{1,0:T(8,128)(2,1)S(1)} %get-tuple-element.70), channel_id=1, source_target_pairs={{0,8},{8,0},{4,12},{12,4},{16,24},{24,16},{20,28},{28,20},{1,9},{9... | collective-permute-start | bytes 245768 | tf_op jit(solution)/shard_map/ppermute | solution.py:55
  5.9 4.2 %collective-permute-start.1 = (bf16[320,128]{1,0:T(8,128)(2,1)S(1)}, bf16[320,128]{1,0:T(8,128)(2,1)S(1)}, u32[]{:S(2)}, u32[]{:S(2)}) collective-permute-start(bf16[320,128]{1,0:T(8,128)(2,1)S(1)} %get-tuple-element.71), channel_id=1, source_target_pairs={{4,8},{8,4},{12,16},{16,12},{20,24},{24,20},{5,9},{9,5},{13,17},{1... | collective-permute-start | bytes 245768 | tf_op jit(solution)/shard_map/ppermute | solution.py:55
  7.3 6.0 %collective-permute-start.3 = (bf16[320,128]{1,0:T(8,128)(2,1)S(1)}, bf16[320,128]{1,0:T(8,128)(2,1)S(1)}, u32[]{:S(2)}, u32[]{:S(2)}) collective-permute-start(bf16[320,128]{1,0:T(8,128)(2,1)S(1)} %get-tuple-element.73), channel_id=1, source_target_pairs={{0,4},{4,0},{8,12},{12,8},{16,20},{20,16},{24,28},{28,24},{1,5},{5... | collective-permute-start | bytes 245768 | tf_op jit(solution)/shard_map/ppermute | solution.py:55
  14.9 9.6 %collective-permute-start.7 = (bf16[256,128]{1,0:T(8,128)(2,1)S(1)}, bf16[256,128]{1,0:T(8,128)(2,1)S(1)}, u32[]{:S(2)}, u32[]{:S(2)}) collective-permute-start(bf16[256,128]{1,0:T(8,128)(2,1)S(1)} %get-tuple-element.85), channel_id=1, source_target_pairs={{8,16},{16,8},{12,20},{20,12},{9,17},{17,9},{13,21},{21,13},{10,18... | collective-permute-start | bytes 196616 | tf_op jit(solution)/shard_map/ppermute | solution.py:62
  15.5 9.5 %collective-permute-start.8 = (bf16[256,128]{1,0:T(8,128)(2,1)S(1)}, bf16[256,128]{1,0:T(8,128)(2,1)S(1)}, u32[]{:S(2)}, u32[]{:S(2)}) collective-permute-start(bf16[256,128]{1,0:T(8,128)(2,1)S(1)} %get-tuple-element.86), channel_id=1, source_target_pairs={{0,8},{8,0},{4,12},{12,4},{16,24},{24,16},{20,28},{28,20},{1,9},{9... | collective-permute-start | bytes 196616 | tf_op jit(solution)/shard_map/ppermute | solution.py:62
  22.8 9.5 %collective-permute-start.10 = (bf16[128,128]{1,0:T(8,128)(2,1)S(1)}, bf16[128,128]{1,0:T(8,128)(2,1)S(1)}, u32[]{:S(2)}, u32[]{:S(2)}) collective-permute-start(bf16[128,128]{1,0:T(8,128)(2,1)S(1)} %get-tuple-element.87), channel_id=1, source_target_pairs={{0,4},{4,0},{8,12},{12,8},{16,20},{20,16},{24,28},{28,24},{1,5},{5... | collective-permute-start | bytes 98312 | tf_op jit(solution)/shard_map/ppermute | solution.py:62
  25.1 7.2 %collective-permute-start.9 = (bf16[128,128]{1,0:T(8,128)(2,1)S(1)}, bf16[128,128]{1,0:T(8,128)(2,1)S(1)}, u32[]{:S(2)}, u32[]{:S(2)}) collective-permute-start(bf16[128,128]{1,0:T(8,128)(2,1)S(1)} %slice_select_fusion.5), channel_id=1, source_target_pairs={{0,4},{4,0},{8,12},{12,8},{16,20},{20,16},{24,28},{28,24},{1,5},{5... | collective-permute-start | bytes 98312 | tf_op jit(solution)/shard_map/ppermute | solution.py:65
  26.8 5.5 %collective-permute-start.4 = (bf16[48,128]{1,0:T(8,128)(2,1)S(1)}, bf16[48,128]{1,0:T(8,128)(2,1)S(1)}, u32[]{:S(2)}, u32[]{:S(2)}) collective-permute-start(bf16[48,128]{1,0:T(8,128)(2,1)S(1)} %get-tuple-element.82), channel_id=1, source_target_pairs={{0,1},{1,2},{2,3},{3,0},{4,5},{5,6},{6,7},{7,4},{8,9},{9,10},{10,1... | collective-permute-start | bytes 36872 | tf_op jit(solution)/shard_map/ppermute | solution.py:489
  26.8 5.5 %collective-permute-start.5 = (bf16[48,128]{1,0:T(8,128)(2,1)S(1)}, bf16[48,128]{1,0:T(8,128)(2,1)S(1)}, u32[]{:S(2)}, u32[]{:S(2)}) collective-permute-start(bf16[48,128]{1,0:T(8,128)(2,1)S(1)} %get-tuple-element.83), channel_id=1, source_target_pairs={{0,2},{1,3},{2,0},{3,1},{4,6},{5,7},{6,4},{7,5},{8,10},{9,11},{10,... | collective-permute-start | bytes 36872 | tf_op jit(solution)/shard_map/ppermute | solution.py:489
  28.3 4.0 %collective-permute-start.6 = (bf16[48,128]{1,0:T(8,128)(2,1)S(1)}, bf16[48,128]{1,0:T(8,128)(2,1)S(1)}, u32[]{:S(2)}, u32[]{:S(2)}) collective-permute-start(bf16[48,128]{1,0:T(8,128)(2,1)S(1)} %get-tuple-element.84), channel_id=1, source_target_pairs={{0,3},{1,0},{2,1},{3,2},{4,7},{5,4},{6,5},{7,6},{8,11},{9,8},{10,9... | collective-permute-start | bytes 36872 | tf_op jit(solution)/shard_map/ppermute | solution.py:489
  33.3 7.7 %collective-permute-start.11 = (bf16[256,128]{1,0:T(8,128)(2,1)S(1)}, bf16[256,128]{1,0:T(8,128)(2,1)S(1)}, u32[]{:S(2)}, u32[]{:S(2)}) collective-permute-start(bf16[256,128]{1,0:T(8,128)(2,1)S(1)} %get-tuple-element.88), channel_id=1, source_target_pairs={{0,8},{8,0},{4,12},{12,4},{16,24},{24,16},{20,28},{28,20},{1,9},{9... | collective-permute-start | bytes 196616 | tf_op jit(solution)/shard_map/ppermute | solution.py:62
  35.4 5.6 %collective-permute-start.12 = (bf16[256,128]{1,0:T(8,128)(2,1)S(1)}, bf16[256,128]{1,0:T(8,128)(2,1)S(1)}, u32[]{:S(2)}, u32[]{:S(2)}) collective-permute-start(bf16[256,128]{1,0:T(8,128)(2,1)S(1)} %get-tuple-element.93), channel_id=1, source_target_pairs={{8,16},{16,8},{12,20},{20,12},{9,17},{17,9},{13,21},{21,13},{10,18... | collective-permute-start | bytes 196616 | tf_op jit(solution)/shard_map/ppermute | solution.py:62
  36.1 11.3 %all-to-all-start = ((f32[32,8,128]{2,1,0:T(8,128)}), f32[32,8,128]{2,1,0:T(8,128)S(1)}, u32[]{:S(2)}, u32[]{:S(2)}) async-start(f32[32,8,128]{2,1,0:T(8,128)} %get-tuple-element.91), calls=%async_computation | async-start | bytes 262144 | tf_op jit(solution)/shard_map/all_to_all | solution.py:493
  39.2 4.2 %collective-permute-start.14 = (bf16[128,128]{1,0:T(8,128)(2,1)S(1)}, bf16[128,128]{1,0:T(8,128)(2,1)S(1)}, u32[]{:S(2)}, u32[]{:S(2)}) collective-permute-start(bf16[128,128]{1,0:T(8,128)(2,1)S(1)} %get-tuple-element.94), channel_id=1, source_target_pairs={{0,4},{4,0},{8,12},{12,8},{16,20},{20,16},{24,28},{28,24},{1,5},{5... | collective-permute-start | bytes 98312 | tf_op jit(solution)/shard_map/ppermute | solution.py:62
  41.0 4.1 %collective-permute-start.13 = (bf16[128,128]{1,0:T(8,128)(2,1)S(1)}, bf16[128,128]{1,0:T(8,128)(2,1)S(1)}, u32[]{:S(2)}, u32[]{:S(2)}) collective-permute-start(bf16[128,128]{1,0:T(8,128)(2,1)S(1)} %slice_select_fusion.4), channel_id=1, source_target_pairs={{0,4},{4,0},{8,12},{12,8},{16,20},{20,16},{24,28},{28,24},{1,5},{5... | collective-permute-start | bytes 98312 | tf_op jit(solution)/shard_map/ppermute | solution.py:65
  60.0 3.7 %collective-permute-start.15 = (bf16[256,128]{1,0:T(8,128)(2,1)S(1)}, bf16[256,128]{1,0:T(8,128)(2,1)S(1)}, u32[]{:S(2)}, u32[]{:S(2)}) collective-permute-start(bf16[256,128]{1,0:T(8,128)(2,1)S(1)} %get-tuple-element.102), channel_id=1, source_target_pairs={{8,16},{16,8},{12,20},{20,12},{9,17},{17,9},{13,21},{21,13},{10,18... | collective-permute-start | bytes 196616 | tf_op jit(solution)/shard_map/ppermute | solution.py:62
  60.7 4.7 %collective-permute-start.16 = (bf16[256,128]{1,0:T(8,128)(2,1)S(1)}, bf16[256,128]{1,0:T(8,128)(2,1)S(1)}, u32[]{:S(2)}, u32[]{:S(2)}) collective-permute-start(bf16[256,128]{1,0:T(8,128)(2,1)S(1)} %get-tuple-element.103), channel_id=1, source_target_pairs={{0,8},{8,0},{4,12},{12,4},{16,24},{24,16},{20,28},{28,20},{1,9},{9... | collective-permute-start | bytes 196616 | tf_op jit(solution)/shard_map/ppermute | solution.py:62
  63.2 5.4 %collective-permute-start.18 = (bf16[128,128]{1,0:T(8,128)(2,1)S(1)}, bf16[128,128]{1,0:T(8,128)(2,1)S(1)}, u32[]{:S(2)}, u32[]{:S(2)}) collective-permute-start(bf16[128,128]{1,0:T(8,128)(2,1)S(1)} %get-tuple-element.104), channel_id=1, source_target_pairs={{0,4},{4,0},{8,12},{12,8},{16,20},{20,16},{24,28},{28,24},{1,5},{5... | collective-permute-start | bytes 98312 | tf_op jit(solution)/shard_map/ppermute | solution.py:62
  65.4 4.0 %collective-permute-start.17 = (bf16[128,128]{1,0:T(8,128)(2,1)S(1)}, bf16[128,128]{1,0:T(8,128)(2,1)S(1)}, u32[]{:S(2)}, u32[]{:S(2)}) collective-permute-start(bf16[128,128]{1,0:T(8,128)(2,1)S(1)} %slice_select_fusion.3), channel_id=1, source_target_pairs={{0,4},{4,0},{8,12},{12,8},{16,20},{20,16},{24,28},{28,24},{1,5},{5... | collective-permute-start | bytes 98312 | tf_op jit(solution)/shard_map/ppermute | solution.py:65
  70.4 7.8 %collective-permute-start.19 = (bf16[256,128]{1,0:T(8,128)(2,1)S(1)}, bf16[256,128]{1,0:T(8,128)(2,1)S(1)}, u32[]{:S(2)}, u32[]{:S(2)}) collective-permute-start(bf16[256,128]{1,0:T(8,128)(2,1)S(1)} %get-tuple-element.105), channel_id=1, source_target_pairs={{0,8},{8,0},{4,12},{12,4},{16,24},{24,16},{20,28},{28,20},{1,9},{9... | collective-permute-start | bytes 196616 | tf_op jit(solution)/shard_map/ppermute | solution.py:62
  72.5 5.7 %collective-permute-start.20 = (bf16[256,128]{1,0:T(8,128)(2,1)S(1)}, bf16[256,128]{1,0:T(8,128)(2,1)S(1)}, u32[]{:S(2)}, u32[]{:S(2)}) collective-permute-start(bf16[256,128]{1,0:T(8,128)(2,1)S(1)} %get-tuple-element.109), channel_id=1, source_target_pairs={{8,16},{16,8},{12,20},{20,12},{9,17},{17,9},{13,21},{21,13},{10,18... | collective-permute-start | bytes 196616 | tf_op jit(solution)/shard_map/ppermute | solution.py:62
  73.2 11.4 %all-to-all-start.2 = ((f32[32,8,128]{2,1,0:T(8,128)}), f32[32,8,128]{2,1,0:T(8,128)S(1)}, u32[]{:S(2)}, u32[]{:S(2)}) async-start(f32[32,8,128]{2,1,0:T(8,128)} %get-tuple-element.108), calls=%async_computation.2 | async-start | bytes 262144 | tf_op jit(solution)/shard_map/all_to_all | solution.py:493
  76.4 4.2 %collective-permute-start.22 = (bf16[128,128]{1,0:T(8,128)(2,1)S(1)}, bf16[128,128]{1,0:T(8,128)(2,1)S(1)}, u32[]{:S(2)}, u32[]{:S(2)}) collective-permute-start(bf16[128,128]{1,0:T(8,128)(2,1)S(1)} %get-tuple-element.110), channel_id=1, source_target_pairs={{0,4},{4,0},{8,12},{12,8},{16,20},{20,16},{24,28},{28,24},{1,5},{5... | collective-permute-start | bytes 98312 | tf_op jit(solution)/shard_map/ppermute | solution.py:62
  78.2 4.1 %collective-permute-start.21 = (bf16[128,128]{1,0:T(8,128)(2,1)S(1)}, bf16[128,128]{1,0:T(8,128)(2,1)S(1)}, u32[]{:S(2)}, u32[]{:S(2)}) collective-permute-start(bf16[128,128]{1,0:T(8,128)(2,1)S(1)} %slice_select_fusion.2), channel_id=1, source_target_pairs={{0,4},{4,0},{8,12},{12,8},{16,20},{20,16},{24,28},{28,24},{1,5},{5... | collective-permute-start | bytes 98312 | tf_op jit(solution)/shard_map/ppermute | solution.py:65
  97.8 4.7 %collective-permute-start.24 = (bf16[256,128]{1,0:T(8,128)(2,1)S(1)}, bf16[256,128]{1,0:T(8,128)(2,1)S(1)}, u32[]{:S(2)}, u32[]{:S(2)}) collective-permute-start(bf16[256,128]{1,0:T(8,128)(2,1)S(1)} %get-tuple-element.118), channel_id=1, source_target_pairs={{0,8},{8,0},{4,12},{12,4},{16,24},{24,16},{20,28},{28,20},{1,9},{9... | collective-permute-start | bytes 196616 | tf_op jit(solution)/shard_map/ppermute | solution.py:62
  100.3 5.4 %collective-permute-start.26 = (bf16[128,128]{1,0:T(8,128)(2,1)S(1)}, bf16[128,128]{1,0:T(8,128)(2,1)S(1)}, u32[]{:S(2)}, u32[]{:S(2)}) collective-permute-start(bf16[128,128]{1,0:T(8,128)(2,1)S(1)} %get-tuple-element.119), channel_id=1, source_target_pairs={{0,4},{4,0},{8,12},{12,8},{16,20},{20,16},{24,28},{28,24},{1,5},{5... | collective-permute-start | bytes 98312 | tf_op jit(solution)/shard_map/ppermute | solution.py:62
  102.6 4.0 %collective-permute-start.25 = (bf16[128,128]{1,0:T(8,128)(2,1)S(1)}, bf16[128,128]{1,0:T(8,128)(2,1)S(1)}, u32[]{:S(2)}, u32[]{:S(2)}) collective-permute-start(bf16[128,128]{1,0:T(8,128)(2,1)S(1)} %slice_select_fusion.1), channel_id=1, source_target_pairs={{0,4},{4,0},{8,12},{12,8},{16,20},{20,16},{24,28},{28,24},{1,5},{5... | collective-permute-start | bytes 98312 | tf_op jit(solution)/shard_map/ppermute | solution.py:65
  107.6 7.8 %collective-permute-start.27 = (bf16[256,128]{1,0:T(8,128)(2,1)S(1)}, bf16[256,128]{1,0:T(8,128)(2,1)S(1)}, u32[]{:S(2)}, u32[]{:S(2)}) collective-permute-start(bf16[256,128]{1,0:T(8,128)(2,1)S(1)} %get-tuple-element.120), channel_id=1, source_target_pairs={{0,8},{8,0},{4,12},{12,4},{16,24},{24,16},{20,28},{28,20},{1,9},{9... | collective-permute-start | bytes 196616 | tf_op jit(solution)/shard_map/ppermute | solution.py:62
  109.7 5.7 %collective-permute-start.28 = (bf16[256,128]{1,0:T(8,128)(2,1)S(1)}, bf16[256,128]{1,0:T(8,128)(2,1)S(1)}, u32[]{:S(2)}, u32[]{:S(2)}) collective-permute-start(bf16[256,128]{1,0:T(8,128)(2,1)S(1)} %get-tuple-element.124), channel_id=1, source_target_pairs={{8,16},{16,8},{12,20},{20,12},{9,17},{17,9},{13,21},{21,13},{10,18... | collective-permute-start | bytes 196616 | tf_op jit(solution)/shard_map/ppermute | solution.py:62
  110.3 11.4 %all-to-all-start.4 = ((f32[32,8,128]{2,1,0:T(8,128)}), f32[32,8,128]{2,1,0:T(8,128)S(1)}, u32[]{:S(2)}, u32[]{:S(2)}) async-start(f32[32,8,128]{2,1,0:T(8,128)} %get-tuple-element.123), calls=%async_computation.4 | async-start | bytes 262144 | tf_op jit(solution)/shard_map/all_to_all | solution.py:493
  113.5 4.2 %collective-permute-start.30 = (bf16[128,128]{1,0:T(8,128)(2,1)S(1)}, bf16[128,128]{1,0:T(8,128)(2,1)S(1)}, u32[]{:S(2)}, u32[]{:S(2)}) collective-permute-start(bf16[128,128]{1,0:T(8,128)(2,1)S(1)} %get-tuple-element.125), channel_id=1, source_target_pairs={{0,4},{4,0},{8,12},{12,8},{16,20},{20,16},{24,28},{28,24},{1,5},{5... | collective-permute-start | bytes 98312 | tf_op jit(solution)/shard_map/ppermute | solution.py:62
  115.4 4.1 %collective-permute-start.29 = (bf16[128,128]{1,0:T(8,128)(2,1)S(1)}, bf16[128,128]{1,0:T(8,128)(2,1)S(1)}, u32[]{:S(2)}, u32[]{:S(2)}) collective-permute-start(bf16[128,128]{1,0:T(8,128)(2,1)S(1)} %slice_select_fusion), channel_id=1, source_target_pairs={{0,4},{4,0},{8,12},{12,8},{16,20},{20,16},{24,28},{28,24},{1,5},{5... | collective-permute-start | bytes 98312 | tf_op jit(solution)/shard_map/ppermute | solution.py:65
  (2 other events, 7.2 us)

commit v2 on v1

--- a/solution.py
+++ b/solution.py
@@ -146,17 +146,18 @@
     return exact(deepen, wide.astype(BF16)).astype(BF16)
 
 
-def start_kernel(faces, steps, groups, pos, offs_h, blks_h, sgns_h, lam_h, modes_h, contact_h, slab_h,
-                 tab, rows_out, own_t, own_slab, *rest):
-    sends, (wide, side, lam, modes, contact, slab, offs, blks, sgns, sems) = rest[:SWAPS], rest[SWAPS:]
+def start_kernel(faces, steps, groups, pos_v, offs_h, blks_h, sgns_h, lam_h, modes_h, contact_h, slab_h,
+                 tab_v, rows_out, own_t, own_slab, *rest):
+    sends, (wide, side, lam, modes, contact, slab, offs, blks, sgns, pos, tab, sems) = rest[:SWAPS], rest[SWAPS:]
     t = Table(faces)
     made = copies(
         ((offs_h, offs), (blks_h, blks), (sgns_h, sgns), (modes_h, modes), (contact_h, contact), (lam_h, lam),
-         (slab_h, slab)), sems)
+         (slab_h, slab), (pos_v, pos)), sems)
     wide[...] = jnp.zeros_like(wide)
     for copy in made:
         copy.wait()
     build_table(faces, tab, pos, offs, blks, sgns)
+    (leave,) = copies(((tab, tab_v),), sems.at[len(made):])
     own_slab[...] = widen_slab(slab, groups)
 
     modes_n = modes.shape[0]
@@ -189,6 +190,7 @@
         for k in range(own_slab.shape[1] // 128):
             here = FIRST_ROWS + k * own_slab.shape[0]
             send[here:here + own_slab.shape[0], :] = own_slab[:, k * 128:(k + 1) * 128]
+    leave.wait()
 
 
 def spread_out(value, out, counts):
@@ -509,19 +511,20 @@
     blocks = -(-(coarse_inverse.shape[1] // modes_n * PAD) // HALF)
     slab_shape = (PAD * n_grp, blocks * 128)
     piece = (COARSE, blocks * 128)
-    pos = jnp.stack([lax.axis_index("sub"), lax.axis_index("grp")]).astype(jnp.int32)
+    lane = jnp.arange(128, dtype=jnp.int32)
+    pos = jnp.where(lane == 0, lax.axis_index("sub"), jnp.where(lane == 1, lax.axis_index("grp"), 0)).astype(jnp.int32)
     flat = hbm(*[a.reshape(n_sub, faces) for a in (face_offset, face_block, face_sign)])
     sent = [((len(held) * block, columns), BF16, VMEM) for held in SENDS]
 
     tab, rows, own_t, own_slab, *sends = call(
         functools.partial(start_kernel, faces, steps, n_grp), "start",
-        [(pos, SMEM)] + flat + hbm(lam_start, modes, contact, coarse_inverse),
-        [((t.size,), jnp.int32, SMEM), ((2 * PAD, order), BF16, VMEM), ((order, 128), BF16, VMEM),
+        vmem(pos) + flat + hbm(lam_start, modes, contact, coarse_inverse),
+        [((t.size,), jnp.int32, VMEM), ((2 * PAD, order), BF16, VMEM), ((order, 128), BF16, VMEM),
          (slab_shape, BF16, VMEM)]
         + [((FIRST_ROWS + slab_shape[0] * slab_shape[1] // 128, columns), BF16, VMEM)] * SWAPS,
         [((128, order), F32), ((order, 128), F32), (lam_start.shape, F32), (modes.shape, F32), (contact.shape, jnp.int32),
          (coarse_inverse.shape, F32)],
-        [((n_sub, faces), jnp.int32)] * 3, 7,
+        [((n_sub, faces), jnp.int32)] * 3 + [((128,), jnp.int32), ((t.size,), jnp.int32)], 9,
     )
     recvs = swap_direct(sends)
     table = [((t.size,), jnp.int32)]

time: 135 us -> 134 us (level)
  no operation moved by 1% of the time
where the time goes in v2:
time: 134 us
  starting transfers between devices  54.3 us (41%)
  blocking collectives  27.9 us (21%)
  waiting for transfers between devices  27 us (20%)
  Pallas kernels  24.1 us (18%)
    ppermute x18, starting transfers between devices, swap_all(): lax.ppermute(send, 'sub', swap_pairs(m, count))  30.7 us
    all_to_all x3, blocking collectives, exchange(): return lax.all_to_all(value, ('sub', 'grp'), 0, 0)  27.9 us
    pallas_call x14, Pallas kernels, call(): pl.pallas_call(kernel, name=name, out_shape=[(HBM if space == HBM else ja...  24.1 us
    ppermute x18, waiting for transfers between devices, swap_all(): lax.ppermute(send, 'sub', swap_pairs(m, count))  9.96 us
    all_to_all x3, starting transfers between devices, exchange(): return lax.all_to_all(value, ('sub', 'grp'), 0, 0)  9.48 us
    ppermute x4, starting transfers between devices, swap_direct(): lax.ppermute(send, 'sub', swap_pairs(m, count))  7.25 us
    ppermute x6, waiting for transfers between devices, swap_all(): lax.ppermute(passed, 'sub', swap_pairs(3, count))  7.06 us
    all_to_all x3, waiting for transfers between devices, exchange(): return lax.all_to_all(value, ('sub', 'grp'), 0, 0)  6.83 us
  transfers between devices with their start and end apart: 34, of which 15 were waited for; matrix products, arithmetic and copies ran while one was open for 0% of the time, Pallas kernels for 6%

profile of v2, /device:TPU:0, one launch (start us, length us, event | category | flops | bytes accessed | tf_op | source)
XLA Modules:
  0.0 133.7 jit_solution(16824763802079916125)
XLA Ops:
  0.0 2.3 %start.1 = (s32[128]{0:T(128)S(1)}, bf16[16,1024]{1,0:T(8,128)(2,1)S(1)}, bf16[1024,128]{1,0:T(8,128)(2,1)S(1)}, bf16[32,128]{1,0:T(8,128)(2,1)S(1)}, bf16[320,1...) custom-call(s32[128]{0:T(128)S(1)} %compare_select_fusion.1.pos_v, ...), custom_call_target="tpu_custom_call" | custom-call | tf_op jit(solution)/shard_map/start/pallas_call | solution.py:467
  2.3 3.1 %collective-permute-start = (bf16[320,128]{1,0:T(8,128)(2,1)S(1)}, bf16[320,128]{1,0:T(8,128)(2,1)S(1)}, u32[]{:S(2)}, u32[]{:S(2)}) collective-permute-start(bf16[320,128]{1,0:T(8,128)(2,1)S(1)} %get-tuple-element.70), channel_id=1, source_target_pairs={{0,8},{8,0},{4,12},{12,4},{16,24},{24,16},{20,28},{28,20},{1,9},{9... | collective-permute-start | bytes 245768 | tf_op jit(solution)/shard_map/ppermute | solution.py:55
  6.7 2.8 %collective-permute-start.3 = (bf16[320,128]{1,0:T(8,128)(2,1)S(1)}, bf16[320,128]{1,0:T(8,128)(2,1)S(1)}, u32[]{:S(2)}, u32[]{:S(2)}) collective-permute-start(bf16[320,128]{1,0:T(8,128)(2,1)S(1)} %get-tuple-element.73), channel_id=1, source_target_pairs={{0,4},{4,0},{8,12},{12,8},{16,20},{20,16},{24,28},{28,24},{1,5},{5... | collective-permute-start | bytes 245768 | tf_op jit(solution)/shard_map/ppermute | solution.py:55
  9.6 3.2 %collective-permute-done.3.rest_3_ = bf16[320,128]{1,0:T(8,128)(2,1)S(1)} collective-permute-done((bf16[320,128]{1,0:T(8,128)(2,1)S(1)}, bf16[320,128]{1,0:T(8,128)(2,1)S(1)}, u32[]{:S(2)}, u32[]{:S(2)}) %collective-permute-start.3) | collective-permute-done | bytes 81952 | tf_op jit(solution)/shard_map/ppermute | solution.py:55
  14.9 7.3 %collective-permute-start.8 = (bf16[256,128]{1,0:T(8,128)(2,1)S(1)}, bf16[256,128]{1,0:T(8,128)(2,1)S(1)}, u32[]{:S(2)}, u32[]{:S(2)}) collective-permute-start(bf16[256,128]{1,0:T(8,128)(2,1)S(1)} %get-tuple-element.86), channel_id=1, source_target_pairs={{0,8},{8,0},{4,12},{12,4},{16,24},{24,16},{20,28},{28,20},{1,9},{9... | collective-permute-start | bytes 196616 | tf_op jit(solution)/shard_map/ppermute | solution.py:62
  29.1 2.5 %inner.3 = (f32[768,128]{1,0:T(8,128)S(1)}, f32[8,128]{1,0:T(8,128)S(1)}) custom-call(bf16[1,1024,1024]{2,1,0:T(8,128)(2,1)} %dual_h.13, f32[1024,128]{1,0:T(8,128)} %loads_h.7, bf16[1024,128]{1,0:T(8,128)(2,1)S(1)} %get-tuple-element.79.zfull, bf16[16,1024]{1,0:T(8,128)(2,1)S(1)} %get-tuple-element.78.rows), custom_call_target="tpu_custom_call" | custom-call | flops 201326592 | bytes 1572864 | tf_op jit(solution)/shard_map/inner/pallas_call | solution.py:467
  32.7 2.1 %collective-permute-start.11 = (bf16[256,128]{1,0:T(8,128)(2,1)S(1)}, bf16[256,128]{1,0:T(8,128)(2,1)S(1)}, u32[]{:S(2)}, u32[]{:S(2)}) collective-permute-start(bf16[256,128]{1,0:T(8,128)(2,1)S(1)} %get-tuple-element.88), channel_id=1, source_target_pairs={{0,8},{8,0},{4,12},{12,4},{16,24},{24,16},{20,28},{28,20},{1,9},{9... | collective-permute-start | bytes 196616 | tf_op jit(solution)/shard_map/ppermute | solution.py:62
  35.5 3.1 %all-to-all-start = ((f32[32,8,128]{2,1,0:T(8,128)}), f32[32,8,128]{2,1,0:T(8,128)S(1)}, u32[]{:S(2)}, u32[]{:S(2)}) async-start(f32[32,8,128]{2,1,0:T(8,128)} %get-tuple-element.91), calls=%async_computation | async-start | bytes 262144 | tf_op jit(solution)/shard_map/all_to_all | solution.py:495
  38.6 1.8 %collective-permute-start.14 = (bf16[128,128]{1,0:T(8,128)(2,1)S(1)}, bf16[128,128]{1,0:T(8,128)(2,1)S(1)}, u32[]{:S(2)}, u32[]{:S(2)}) collective-permute-start(bf16[128,128]{1,0:T(8,128)(2,1)S(1)} %get-tuple-element.94), channel_id=1, source_target_pairs={{0,4},{4,0},{8,12},{12,8},{16,20},{20,16},{24,28},{28,24},{1,5},{5... | collective-permute-start | bytes 98312 | tf_op jit(solution)/shard_map/ppermute | solution.py:62
  40.8 2.0 %collective-permute-done.14.rest_2_ = bf16[128,128]{1,0:T(8,128)(2,1)S(1)} collective-permute-done((bf16[128,128]{1,0:T(8,128)(2,1)S(1)}, bf16[128,128]{1,0:T(8,128)(2,1)S(1)}, u32[]{:S(2)}, u32[]{:S(2)}) %collective-permute-start.14) | collective-permute-done | bytes 32800 | tf_op jit(solution)/shard_map/ppermute | solution.py:62
  42.8 1.8 %collective-permute-done.13.rest_1_ = bf16[128,128]{1,0:T(8,128)(2,1)S(1)} collective-permute-done((bf16[128,128]{1,0:T(8,128)(2,1)S(1)}, bf16[128,128]{1,0:T(8,128)(2,1)S(1)}, u32[]{:S(2)}, u32[]{:S(2)}) %collective-permute-start.13) | collective-permute-done | bytes 32800 | tf_op jit(solution)/shard_map/ppermute | solution.py:65
  44.6 2.3 %all-to-all-done.every = f32[32,8,128]{2,1,0:T(8,128)S(1)} async-done(((f32[32,8,128]{2,1,0:T(8,128)}), f32[32,8,128]{2,1,0:T(8,128)S(1)}, u32[]{:S(2)}, u32[]{:S(2)}) %all-to-all-start) | async-done | bytes 131104 | tf_op jit(solution)/shard_map/all_to_all | solution.py:495
  46.8 2.2 %direction.3 = (f32[1280,128]{1,0:T(8,128)S(1)}, f32[32,2,128]{2,1,0:T(2,128)S(1)}) custom-call(s32[128]{0:T(128)S(1)} %get-tuple-element.67.tab_v, bf16[1,1024,1024]{2,1,0:T(8,128)(2,1)} %dual_h.13, bf16[256,1024]{1,0:T(8,128)(2,1)S(1)} %get-tuple-element.74.dual, bf16[256,128]{1,0:T(8,128)(2,1)S(1)} %collective-permute-done.11.near, ...), custom_call_target="tpu_custom_call" | custom-call | tf_op jit(solution)/shard_map/direction/pallas_call | solution.py:467
  49.1 9.3 %all_to_all.30.parts = f32[32,2,128]{2,1,0:T(2,128)S(1)} all-to-all(f32[32,2,128]{2,1,0:T(2,128)S(1)} %get-tuple-element.96), channel_id=1, replica_groups=mesh['sub'=8,'grp'=4] {'sub','grp'}, dimensions={0} | all-to-all | bytes 65536 | tf_op jit(solution)/shard_map/all_to_all | solution.py:495
  60.1 2.5 %collective-permute-start.16 = (bf16[256,128]{1,0:T(8,128)(2,1)S(1)}, bf16[256,128]{1,0:T(8,128)(2,1)S(1)}, u32[]{:S(2)}, u32[]{:S(2)}) collective-permute-start(bf16[256,128]{1,0:T(8,128)(2,1)S(1)} %get-tuple-element.103), channel_id=1, source_target_pairs={{0,8},{8,0},{4,12},{12,4},{16,24},{24,16},{20,28},{28,20},{1,9},{9... | collective-permute-start | bytes 196616 | tf_op jit(solution)/shard_map/ppermute | solution.py:62
  65.4 2.5 %inner.4 = (f32[768,128]{1,0:T(8,128)S(1)}, f32[8,128]{1,0:T(8,128)S(1)}) custom-call(bf16[1,1024,1024]{2,1,0:T(8,128)(2,1)} %dual_h.13, f32[1024,128]{1,0:T(8,128)} %loads_h.7, bf16[1024,128]{1,0:T(8,128)(2,1)S(1)} %get-tuple-element.100.zfull, bf16[16,1024]{1,0:T(8,128)(2,1)S(1)} %get-tuple-element.78.rows), custom_call_target="tpu_custom_call" | custom-call | flops 201326592 | bytes 1572864 | tf_op jit(solution)/shard_map/inner/pallas_call | solution.py:467
  69.8 2.1 %collective-permute-start.19 = (bf16[256,128]{1,0:T(8,128)(2,1)S(1)}, bf16[256,128]{1,0:T(8,128)(2,1)S(1)}, u32[]{:S(2)}, u32[]{:S(2)}) collective-permute-start(bf16[256,128]{1,0:T(8,128)(2,1)S(1)} %get-tuple-element.105), channel_id=1, source_target_pairs={{0,8},{8,0},{4,12},{12,4},{16,24},{24,16},{20,28},{28,20},{1,9},{9... | collective-permute-start | bytes 196616 | tf_op jit(solution)/shard_map/ppermute | solution.py:62
  72.6 3.2 %all-to-all-start.2 = ((f32[32,8,128]{2,1,0:T(8,128)}), f32[32,8,128]{2,1,0:T(8,128)S(1)}, u32[]{:S(2)}, u32[]{:S(2)}) async-start(f32[32,8,128]{2,1,0:T(8,128)} %get-tuple-element.108), calls=%async_computation.2 | async-start | bytes 262144 | tf_op jit(solution)/shard_map/all_to_all | solution.py:495
  75.8 1.8 %collective-permute-start.22 = (bf16[128,128]{1,0:T(8,128)(2,1)S(1)}, bf16[128,128]{1,0:T(8,128)(2,1)S(1)}, u32[]{:S(2)}, u32[]{:S(2)}) collective-permute-start(bf16[128,128]{1,0:T(8,128)(2,1)S(1)} %get-tuple-element.110), channel_id=1, source_target_pairs={{0,4},{4,0},{8,12},{12,8},{16,20},{20,16},{24,28},{28,24},{1,5},{5... | collective-permute-start | bytes 98312 | tf_op jit(solution)/shard_map/ppermute | solution.py:62
  78.0 2.0 %collective-permute-done.22.rest_2_ = bf16[128,128]{1,0:T(8,128)(2,1)S(1)} collective-permute-done((bf16[128,128]{1,0:T(8,128)(2,1)S(1)}, bf16[128,128]{1,0:T(8,128)(2,1)S(1)}, u32[]{:S(2)}, u32[]{:S(2)}) %collective-permute-start.22) | collective-permute-done | bytes 32800 | tf_op jit(solution)/shard_map/ppermute | solution.py:62
  81.7 2.3 %all-to-all-done.2.every = f32[32,8,128]{2,1,0:T(8,128)S(1)} async-done(((f32[32,8,128]{2,1,0:T(8,128)}), f32[32,8,128]{2,1,0:T(8,128)S(1)}, u32[]{:S(2)}, u32[]{:S(2)}) %all-to-all-start.2) | async-done | bytes 131104 | tf_op jit(solution)/shard_map/all_to_all | solution.py:495
  84.0 2.2 %direction.4 = (f32[1280,128]{1,0:T(8,128)S(1)}, f32[32,2,128]{2,1,0:T(2,128)S(1)}) custom-call(s32[128]{0:T(128)S(1)} %get-tuple-element.67.tab_v, bf16[1,1024,1024]{2,1,0:T(8,128)(2,1)} %dual_h.13, bf16[256,1024]{1,0:T(8,128)(2,1)S(1)} %get-tuple-element.74.dual, bf16[256,128]{1,0:T(8,128)(2,1)S(1)} %collective-permute-done.19.near, ...), custom_call_target="tpu_custom_call" | custom-call | tf_op jit(solution)/shard_map/direction/pallas_call | solution.py:467
  86.2 9.3 %all_to_all.31.parts = f32[32,2,128]{2,1,0:T(2,128)S(1)} all-to-all(f32[32,2,128]{2,1,0:T(2,128)S(1)} %get-tuple-element.111), channel_id=1, replica_groups=mesh['sub'=8,'grp'=4] {'sub','grp'}, dimensions={0} | all-to-all | bytes 65536 | tf_op jit(solution)/shard_map/all_to_all | solution.py:495
  97.3 2.5 %collective-permute-start.24 = (bf16[256,128]{1,0:T(8,128)(2,1)S(1)}, bf16[256,128]{1,0:T(8,128)(2,1)S(1)}, u32[]{:S(2)}, u32[]{:S(2)}) collective-permute-start(bf16[256,128]{1,0:T(8,128)(2,1)S(1)} %get-tuple-element.118), channel_id=1, source_target_pairs={{0,8},{8,0},{4,12},{12,4},{16,24},{24,16},{20,28},{28,20},{1,9},{9... | collective-permute-start | bytes 196616 | tf_op jit(solution)/shard_map/ppermute | solution.py:62
  102.6 2.5 %inner.5 = (f32[768,128]{1,0:T(8,128)S(1)}, f32[8,128]{1,0:T(8,128)S(1)}) custom-call(bf16[1,1024,1024]{2,1,0:T(8,128)(2,1)} %dual_h.13, f32[1024,128]{1,0:T(8,128)} %loads_h.7, bf16[1024,128]{1,0:T(8,128)(2,1)S(1)} %get-tuple-element.115.zfull, bf16[16,1024]{1,0:T(8,128)(2,1)S(1)} %get-tuple-element.78.rows), custom_call_target="tpu_custom_call" | custom-call | flops 201326592 | bytes 1572864 | tf_op jit(solution)/shard_map/inner/pallas_call | solution.py:467
  107.0 2.1 %collective-permute-start.27 = (bf16[256,128]{1,0:T(8,128)(2,1)S(1)}, bf16[256,128]{1,0:T(8,128)(2,1)S(1)}, u32[]{:S(2)}, u32[]{:S(2)}) collective-permute-start(bf16[256,128]{1,0:T(8,128)(2,1)S(1)} %get-tuple-element.120), channel_id=1, source_target_pairs={{0,8},{8,0},{4,12},{12,4},{16,24},{24,16},{20,28},{28,20},{1,9},{9... | collective-permute-start | bytes 196616 | tf_op jit(solution)/shard_map/ppermute | solution.py:62
  109.8 3.2 %all-to-all-start.4 = ((f32[32,8,128]{2,1,0:T(8,128)}), f32[32,8,128]{2,1,0:T(8,128)S(1)}, u32[]{:S(2)}, u32[]{:S(2)}) async-start(f32[32,8,128]{2,1,0:T(8,128)} %get-tuple-element.123), calls=%async_computation.4 | async-start | bytes 262144 | tf_op jit(solution)/shard_map/all_to_all | solution.py:495
  113.0 1.8 %collective-permute-start.30 = (bf16[128,128]{1,0:T(8,128)(2,1)S(1)}, bf16[128,128]{1,0:T(8,128)(2,1)S(1)}, u32[]{:S(2)}, u32[]{:S(2)}) collective-permute-start(bf16[128,128]{1,0:T(8,128)(2,1)S(1)} %get-tuple-element.125), channel_id=1, source_target_pairs={{0,4},{4,0},{8,12},{12,8},{16,20},{20,16},{24,28},{28,24},{1,5},{5... | collective-permute-start | bytes 98312 | tf_op jit(solution)/shard_map/ppermute | solution.py:62
  115.1 2.0 %collective-permute-done.30.rest_2_ = bf16[128,128]{1,0:T(8,128)(2,1)S(1)} collective-permute-done((bf16[128,128]{1,0:T(8,128)(2,1)S(1)}, bf16[128,128]{1,0:T(8,128)(2,1)S(1)}, u32[]{:S(2)}, u32[]{:S(2)}) %collective-permute-start.30) | collective-permute-done | bytes 32800 | tf_op jit(solution)/shard_map/ppermute | solution.py:62
  118.9 2.3 %all-to-all-done.4.every = f32[32,8,128]{2,1,0:T(8,128)S(1)} async-done(((f32[32,8,128]{2,1,0:T(8,128)}), f32[32,8,128]{2,1,0:T(8,128)S(1)}, u32[]{:S(2)}, u32[]{:S(2)}) %all-to-all-start.4) | async-done | bytes 131104 | tf_op jit(solution)/shard_map/all_to_all | solution.py:495
  121.2 2.2 %direction.5 = (f32[1280,128]{1,0:T(8,128)S(1)}, f32[32,2,128]{2,1,0:T(2,128)S(1)}) custom-call(s32[128]{0:T(128)S(1)} %get-tuple-element.67.tab_v, bf16[1,1024,1024]{2,1,0:T(8,128)(2,1)} %dual_h.13, bf16[256,1024]{1,0:T(8,128)(2,1)S(1)} %get-tuple-element.74.dual, bf16[256,128]{1,0:T(8,128)(2,1)S(1)} %collective-permute-done.27.near, ...), custom_call_target="tpu_custom_call" | custom-call | tf_op jit(solution)/shard_map/direction/pallas_call | solution.py:467
  123.4 9.3 %all_to_all.32.parts = f32[32,2,128]{2,1,0:T(2,128)S(1)} all-to-all(f32[32,2,128]{2,1,0:T(2,128)S(1)} %get-tuple-element.126), channel_id=1, replica_groups=mesh['sub'=8,'grp'=4] {'sub','grp'}, dimensions={0} | all-to-all | bytes 65536 | tf_op jit(solution)/shard_map/all_to_all | solution.py:495
  (60 shorter events, 31.8 us)
Async XLA Ops:
  2.3 7.3 %collective-permute-start = (bf16[320,128]{1,0:T(8,128)(2,1)S(1)}, bf16[320,128]{1,0:T(8,128)(2,1)S(1)}, u32[]{:S(2)}, u32[]{:S(2)}) collective-permute-start(bf16[320,128]{1,0:T(8,128)(2,1)S(1)} %get-tuple-element.70), channel_id=1, source_target_pairs={{0,8},{8,0},{4,12},{12,4},{16,24},{24,16},{20,28},{28,20},{1,9},{9... | collective-permute-start | bytes 245768 | tf_op jit(solution)/shard_map/ppermute | solution.py:55
  5.4 4.2 %collective-permute-start.1 = (bf16[320,128]{1,0:T(8,128)(2,1)S(1)}, bf16[320,128]{1,0:T(8,128)(2,1)S(1)}, u32[]{:S(2)}, u32[]{:S(2)}) collective-permute-start(bf16[320,128]{1,0:T(8,128)(2,1)S(1)} %get-tuple-element.71), channel_id=1, source_target_pairs={{4,8},{8,4},{12,16},{16,12},{20,24},{24,20},{5,9},{9,5},{13,17},{1... | collective-permute-start | bytes 245768 | tf_op jit(solution)/shard_map/ppermute | solution.py:55
  6.7 6.0 %collective-permute-start.3 = (bf16[320,128]{1,0:T(8,128)(2,1)S(1)}, bf16[320,128]{1,0:T(8,128)(2,1)S(1)}, u32[]{:S(2)}, u32[]{:S(2)}) collective-permute-start(bf16[320,128]{1,0:T(8,128)(2,1)S(1)} %get-tuple-element.73), channel_id=1, source_target_pairs={{0,4},{4,0},{8,12},{12,8},{16,20},{20,16},{24,28},{28,24},{1,5},{5... | collective-permute-start | bytes 245768 | tf_op jit(solution)/shard_map/ppermute | solution.py:55
  14.3 9.6 %collective-permute-start.7 = (bf16[256,128]{1,0:T(8,128)(2,1)S(1)}, bf16[256,128]{1,0:T(8,128)(2,1)S(1)}, u32[]{:S(2)}, u32[]{:S(2)}) collective-permute-start(bf16[256,128]{1,0:T(8,128)(2,1)S(1)} %get-tuple-element.85), channel_id=1, source_target_pairs={{8,16},{16,8},{12,20},{20,12},{9,17},{17,9},{13,21},{21,13},{10,18... | collective-permute-start | bytes 196616 | tf_op jit(solution)/shard_map/ppermute | solution.py:62
  14.9 9.5 %collective-permute-start.8 = (bf16[256,128]{1,0:T(8,128)(2,1)S(1)}, bf16[256,128]{1,0:T(8,128)(2,1)S(1)}, u32[]{:S(2)}, u32[]{:S(2)}) collective-permute-start(bf16[256,128]{1,0:T(8,128)(2,1)S(1)} %get-tuple-element.86), channel_id=1, source_target_pairs={{0,8},{8,0},{4,12},{12,4},{16,24},{24,16},{20,28},{28,20},{1,9},{9... | collective-permute-start | bytes 196616 | tf_op jit(solution)/shard_map/ppermute | solution.py:62
  22.2 9.5 %collective-permute-start.10 = (bf16[128,128]{1,0:T(8,128)(2,1)S(1)}, bf16[128,128]{1,0:T(8,128)(2,1)S(1)}, u32[]{:S(2)}, u32[]{:S(2)}) collective-permute-start(bf16[128,128]{1,0:T(8,128)(2,1)S(1)} %get-tuple-element.87), channel_id=1, source_target_pairs={{0,4},{4,0},{8,12},{12,8},{16,20},{20,16},{24,28},{28,24},{1,5},{5... | collective-permute-start | bytes 98312 | tf_op jit(solution)/shard_map/ppermute | solution.py:62
  24.5 7.2 %collective-permute-start.9 = (bf16[128,128]{1,0:T(8,128)(2,1)S(1)}, bf16[128,128]{1,0:T(8,128)(2,1)S(1)}, u32[]{:S(2)}, u32[]{:S(2)}) collective-permute-start(bf16[128,128]{1,0:T(8,128)(2,1)S(1)} %slice_select_fusion.5), channel_id=1, source_target_pairs={{0,4},{4,0},{8,12},{12,8},{16,20},{20,16},{24,28},{28,24},{1,5},{5... | collective-permute-start | bytes 98312 | tf_op jit(solution)/shard_map/ppermute | solution.py:65
  26.2 5.5 %collective-permute-start.4 = (bf16[48,128]{1,0:T(8,128)(2,1)S(1)}, bf16[48,128]{1,0:T(8,128)(2,1)S(1)}, u32[]{:S(2)}, u32[]{:S(2)}) collective-permute-start(bf16[48,128]{1,0:T(8,128)(2,1)S(1)} %get-tuple-element.82), channel_id=1, source_target_pairs={{0,1},{1,2},{2,3},{3,0},{4,5},{5,6},{6,7},{7,4},{8,9},{9,10},{10,1... | collective-permute-start | bytes 36872 | tf_op jit(solution)/shard_map/ppermute | solution.py:491
  26.2 5.5 %collective-permute-start.5 = (bf16[48,128]{1,0:T(8,128)(2,1)S(1)}, bf16[48,128]{1,0:T(8,128)(2,1)S(1)}, u32[]{:S(2)}, u32[]{:S(2)}) collective-permute-start(bf16[48,128]{1,0:T(8,128)(2,1)S(1)} %get-tuple-element.83), channel_id=1, source_target_pairs={{0,2},{1,3},{2,0},{3,1},{4,6},{5,7},{6,4},{7,5},{8,10},{9,11},{10,... | collective-permute-start | bytes 36872 | tf_op jit(solution)/shard_map/ppermute | solution.py:491
  27.7 4.0 %collective-permute-start.6 = (bf16[48,128]{1,0:T(8,128)(2,1)S(1)}, bf16[48,128]{1,0:T(8,128)(2,1)S(1)}, u32[]{:S(2)}, u32[]{:S(2)}) collective-permute-start(bf16[48,128]{1,0:T(8,128)(2,1)S(1)} %get-tuple-element.84), channel_id=1, source_target_pairs={{0,3},{1,0},{2,1},{3,2},{4,7},{5,4},{6,5},{7,6},{8,11},{9,8},{10,9... | collective-permute-start | bytes 36872 | tf_op jit(solution)/shard_map/ppermute | solution.py:491
  32.7 7.7 %collective-permute-start.11 = (bf16[256,128]{1,0:T(8,128)(2,1)S(1)}, bf16[256,128]{1,0:T(8,128)(2,1)S(1)}, u32[]{:S(2)}, u32[]{:S(2)}) collective-permute-start(bf16[256,128]{1,0:T(8,128)(2,1)S(1)} %get-tuple-element.88), channel_id=1, source_target_pairs={{0,8},{8,0},{4,12},{12,4},{16,24},{24,16},{20,28},{28,20},{1,9},{9... | collective-permute-start | bytes 196616 | tf_op jit(solution)/shard_map/ppermute | solution.py:62
  34.8 5.6 %collective-permute-start.12 = (bf16[256,128]{1,0:T(8,128)(2,1)S(1)}, bf16[256,128]{1,0:T(8,128)(2,1)S(1)}, u32[]{:S(2)}, u32[]{:S(2)}) collective-permute-start(bf16[256,128]{1,0:T(8,128)(2,1)S(1)} %get-tuple-element.93), channel_id=1, source_target_pairs={{8,16},{16,8},{12,20},{20,12},{9,17},{17,9},{13,21},{21,13},{10,18... | collective-permute-start | bytes 196616 | tf_op jit(solution)/shard_map/ppermute | solution.py:62
  35.5 11.3 %all-to-all-start = ((f32[32,8,128]{2,1,0:T(8,128)}), f32[32,8,128]{2,1,0:T(8,128)S(1)}, u32[]{:S(2)}, u32[]{:S(2)}) async-start(f32[32,8,128]{2,1,0:T(8,128)} %get-tuple-element.91), calls=%async_computation | async-start | bytes 262144 | tf_op jit(solution)/shard_map/all_to_all | solution.py:495
  38.6 4.2 %collective-permute-start.14 = (bf16[128,128]{1,0:T(8,128)(2,1)S(1)}, bf16[128,128]{1,0:T(8,128)(2,1)S(1)}, u32[]{:S(2)}, u32[]{:S(2)}) collective-permute-start(bf16[128,128]{1,0:T(8,128)(2,1)S(1)} %get-tuple-element.94), channel_id=1, source_target_pairs={{0,4},{4,0},{8,12},{12,8},{16,20},{20,16},{24,28},{28,24},{1,5},{5... | collective-permute-start | bytes 98312 | tf_op jit(solution)/shard_map/ppermute | solution.py:62
  40.5 4.1 %collective-permute-start.13 = (bf16[128,128]{1,0:T(8,128)(2,1)S(1)}, bf16[128,128]{1,0:T(8,128)(2,1)S(1)}, u32[]{:S(2)}, u32[]{:S(2)}) collective-permute-start(bf16[128,128]{1,0:T(8,128)(2,1)S(1)} %slice_select_fusion.4), channel_id=1, source_target_pairs={{0,4},{4,0},{8,12},{12,8},{16,20},{20,16},{24,28},{28,24},{1,5},{5... | collective-permute-start | bytes 98312 | tf_op jit(solution)/shard_map/ppermute | solution.py:65
  59.4 3.7 %collective-permute-start.15 = (bf16[256,128]{1,0:T(8,128)(2,1)S(1)}, bf16[256,128]{1,0:T(8,128)(2,1)S(1)}, u32[]{:S(2)}, u32[]{:S(2)}) collective-permute-start(bf16[256,128]{1,0:T(8,128)(2,1)S(1)} %get-tuple-element.102), channel_id=1, source_target_pairs={{8,16},{16,8},{12,20},{20,12},{9,17},{17,9},{13,21},{21,13},{10,18... | collective-permute-start | bytes 196616 | tf_op jit(solution)/shard_map/ppermute | solution.py:62
  60.1 4.7 %collective-permute-start.16 = (bf16[256,128]{1,0:T(8,128)(2,1)S(1)}, bf16[256,128]{1,0:T(8,128)(2,1)S(1)}, u32[]{:S(2)}, u32[]{:S(2)}) collective-permute-start(bf16[256,128]{1,0:T(8,128)(2,1)S(1)} %get-tuple-element.103), channel_id=1, source_target_pairs={{0,8},{8,0},{4,12},{12,4},{16,24},{24,16},{20,28},{28,20},{1,9},{9... | collective-permute-start | bytes 196616 | tf_op jit(solution)/shard_map/ppermute | solution.py:62
  62.6 5.4 %collective-permute-start.18 = (bf16[128,128]{1,0:T(8,128)(2,1)S(1)}, bf16[128,128]{1,0:T(8,128)(2,1)S(1)}, u32[]{:S(2)}, u32[]{:S(2)}) collective-permute-start(bf16[128,128]{1,0:T(8,128)(2,1)S(1)} %get-tuple-element.104), channel_id=1, source_target_pairs={{0,4},{4,0},{8,12},{12,8},{16,20},{20,16},{24,28},{28,24},{1,5},{5... | collective-permute-start | bytes 98312 | tf_op jit(solution)/shard_map/ppermute | solution.py:62
  64.8 4.0 %collective-permute-start.17 = (bf16[128,128]{1,0:T(8,128)(2,1)S(1)}, bf16[128,128]{1,0:T(8,128)(2,1)S(1)}, u32[]{:S(2)}, u32[]{:S(2)}) collective-permute-start(bf16[128,128]{1,0:T(8,128)(2,1)S(1)} %slice_select_fusion.3), channel_id=1, source_target_pairs={{0,4},{4,0},{8,12},{12,8},{16,20},{20,16},{24,28},{28,24},{1,5},{5... | collective-permute-start | bytes 98312 | tf_op jit(solution)/shard_map/ppermute | solution.py:65
  69.8 7.8 %collective-permute-start.19 = (bf16[256,128]{1,0:T(8,128)(2,1)S(1)}, bf16[256,128]{1,0:T(8,128)(2,1)S(1)}, u32[]{:S(2)}, u32[]{:S(2)}) collective-permute-start(bf16[256,128]{1,0:T(8,128)(2,1)S(1)} %get-tuple-element.105), channel_id=1, source_target_pairs={{0,8},{8,0},{4,12},{12,4},{16,24},{24,16},{20,28},{28,20},{1,9},{9... | collective-permute-start | bytes 196616 | tf_op jit(solution)/shard_map/ppermute | solution.py:62
  71.9 5.7 %collective-permute-start.20 = (bf16[256,128]{1,0:T(8,128)(2,1)S(1)}, bf16[256,128]{1,0:T(8,128)(2,1)S(1)}, u32[]{:S(2)}, u32[]{:S(2)}) collective-permute-start(bf16[256,128]{1,0:T(8,128)(2,1)S(1)} %get-tuple-element.109), channel_id=1, source_target_pairs={{8,16},{16,8},{12,20},{20,12},{9,17},{17,9},{13,21},{21,13},{10,18... | collective-permute-start | bytes 196616 | tf_op jit(solution)/shard_map/ppermute | solution.py:62
  72.6 11.4 %all-to-all-start.2 = ((f32[32,8,128]{2,1,0:T(8,128)}), f32[32,8,128]{2,1,0:T(8,128)S(1)}, u32[]{:S(2)}, u32[]{:S(2)}) async-start(f32[32,8,128]{2,1,0:T(8,128)} %get-tuple-element.108), calls=%async_computation.2 | async-start | bytes 262144 | tf_op jit(solution)/shard_map/all_to_all | solution.py:495
  75.8 4.2 %collective-permute-start.22 = (bf16[128,128]{1,0:T(8,128)(2,1)S(1)}, bf16[128,128]{1,0:T(8,128)(2,1)S(1)}, u32[]{:S(2)}, u32[]{:S(2)}) collective-permute-start(bf16[128,128]{1,0:T(8,128)(2,1)S(1)} %get-tuple-element.110), channel_id=1, source_target_pairs={{0,4},{4,0},{8,12},{12,8},{16,20},{20,16},{24,28},{28,24},{1,5},{5... | collective-permute-start | bytes 98312 | tf_op jit(solution)/shard_map/ppermute | solution.py:62
  77.6 4.1 %collective-permute-start.21 = (bf16[128,128]{1,0:T(8,128)(2,1)S(1)}, bf16[128,128]{1,0:T(8,128)(2,1)S(1)}, u32[]{:S(2)}, u32[]{:S(2)}) collective-permute-start(bf16[128,128]{1,0:T(8,128)(2,1)S(1)} %slice_select_fusion.2), channel_id=1, source_target_pairs={{0,4},{4,0},{8,12},{12,8},{16,20},{20,16},{24,28},{28,24},{1,5},{5... | collective-permute-start | bytes 98312 | tf_op jit(solution)/shard_map/ppermute | solution.py:65
  97.3 4.7 %collective-permute-start.24 = (bf16[256,128]{1,0:T(8,128)(2,1)S(1)}, bf16[256,128]{1,0:T(8,128)(2,1)S(1)}, u32[]{:S(2)}, u32[]{:S(2)}) collective-permute-start(bf16[256,128]{1,0:T(8,128)(2,1)S(1)} %get-tuple-element.118), channel_id=1, source_target_pairs={{0,8},{8,0},{4,12},{12,4},{16,24},{24,16},{20,28},{28,20},{1,9},{9... | collective-permute-start | bytes 196616 | tf_op jit(solution)/shard_map/ppermute | solution.py:62
  99.8 5.4 %collective-permute-start.26 = (bf16[128,128]{1,0:T(8,128)(2,1)S(1)}, bf16[128,128]{1,0:T(8,128)(2,1)S(1)}, u32[]{:S(2)}, u32[]{:S(2)}) collective-permute-start(bf16[128,128]{1,0:T(8,128)(2,1)S(1)} %get-tuple-element.119), channel_id=1, source_target_pairs={{0,4},{4,0},{8,12},{12,8},{16,20},{20,16},{24,28},{28,24},{1,5},{5... | collective-permute-start | bytes 98312 | tf_op jit(solution)/shard_map/ppermute | solution.py:62
  102.0 4.0 %collective-permute-start.25 = (bf16[128,128]{1,0:T(8,128)(2,1)S(1)}, bf16[128,128]{1,0:T(8,128)(2,1)S(1)}, u32[]{:S(2)}, u32[]{:S(2)}) collective-permute-start(bf16[128,128]{1,0:T(8,128)(2,1)S(1)} %slice_select_fusion.1), channel_id=1, source_target_pairs={{0,4},{4,0},{8,12},{12,8},{16,20},{20,16},{24,28},{28,24},{1,5},{5... | collective-permute-start | bytes 98312 | tf_op jit(solution)/shard_map/ppermute | solution.py:65
  107.0 7.8 %collective-permute-start.27 = (bf16[256,128]{1,0:T(8,128)(2,1)S(1)}, bf16[256,128]{1,0:T(8,128)(2,1)S(1)}, u32[]{:S(2)}, u32[]{:S(2)}) collective-permute-start(bf16[256,128]{1,0:T(8,128)(2,1)S(1)} %get-tuple-element.120), channel_id=1, source_target_pairs={{0,8},{8,0},{4,12},{12,4},{16,24},{24,16},{20,28},{28,20},{1,9},{9... | collective-permute-start | bytes 196616 | tf_op jit(solution)/shard_map/ppermute | solution.py:62
  109.1 5.7 %collective-permute-start.28 = (bf16[256,128]{1,0:T(8,128)(2,1)S(1)}, bf16[256,128]{1,0:T(8,128)(2,1)S(1)}, u32[]{:S(2)}, u32[]{:S(2)}) collective-permute-start(bf16[256,128]{1,0:T(8,128)(2,1)S(1)} %get-tuple-element.124), channel_id=1, source_target_pairs={{8,16},{16,8},{12,20},{20,12},{9,17},{17,9},{13,21},{21,13},{10,18... | collective-permute-start | bytes 196616 | tf_op jit(solution)/shard_map/ppermute | solution.py:62
  109.8 11.4 %all-to-all-start.4 = ((f32[32,8,128]{2,1,0:T(8,128)}), f32[32,8,128]{2,1,0:T(8,128)S(1)}, u32[]{:S(2)}, u32[]{:S(2)}) async-start(f32[32,8,128]{2,1,0:T(8,128)} %get-tuple-element.123), calls=%async_computation.4 | async-start | bytes 262144 | tf_op jit(solution)/shard_map/all_to_all | solution.py:495
  113.0 4.2 %collective-permute-start.30 = (bf16[128,128]{1,0:T(8,128)(2,1)S(1)}, bf16[128,128]{1,0:T(8,128)(2,1)S(1)}, u32[]{:S(2)}, u32[]{:S(2)}) collective-permute-start(bf16[128,128]{1,0:T(8,128)(2,1)S(1)} %get-tuple-element.125), channel_id=1, source_target_pairs={{0,4},{4,0},{8,12},{12,8},{16,20},{20,16},{24,28},{28,24},{1,5},{5... | collective-permute-start | bytes 98312 | tf_op jit(solution)/shard_map/ppermute | solution.py:62
  114.8 4.1 %collective-permute-start.29 = (bf16[128,128]{1,0:T(8,128)(2,1)S(1)}, bf16[128,128]{1,0:T(8,128)(2,1)S(1)}, u32[]{:S(2)}, u32[]{:S(2)}) collective-permute-start(bf16[128,128]{1,0:T(8,128)(2,1)S(1)} %slice_select_fusion), channel_id=1, source_target_pairs={{0,4},{4,0},{8,12},{12,8},{16,20},{20,16},{24,28},{28,24},{1,5},{5... | collective-permute-start | bytes 98312 | tf_op jit(solution)/shard_map/ppermute | solution.py:65
  (2 other events, 7.2 us)

commit v3 on v2

--- a/solution.py
+++ b/solution.py
@@ -411,12 +411,6 @@
     order = grad.shape[0] + grad_in.shape[0]
     face_rows = faces * FACE_ROWS
     block = CAP * FACE_ROWS
-    for m, recv in enumerate(recvs):
-        joined[m * block:(m + 1) * block, :] = recv[0:block, :]
-    enter.wait()
-    for f in range(faces):
-        at = f * FACE_ROWS
-        grad_all[at:at + FACE_ROWS, :] = joined[rows_of(tab[t.slot + f]), :].astype(F32)
     residual = every[...].reshape(every.shape[0] * PAD, columns)
     high, low = split(residual)
     stacked = jnp.concatenate([high, low, high], axis=0)
@@ -428,9 +422,15 @@
     pieces.append(jnp.zeros((all_t.shape[1] - CONTACT_LANE, columns), F32))
     weights = jnp.concatenate(pieces, axis=0).astype(BF16)
     shift = jnp.dot(all_t[...], weights, preferred_element_type=F32)
-    dirn[order:, :] = grad_all[...] - shift[order:, :]
     dirn[0:face_rows, :] = grad[...] - shift[0:face_rows, :]
     dirn[face_rows:order, :] = grad_in[...] - shift[face_rows:order, :]
+    for m, recv in enumerate(recvs):
+        joined[m * block:(m + 1) * block, :] = recv[0:block, :]
+    enter.wait()
+    for f in range(faces):
+        at = f * FACE_ROWS
+        grad_all[at:at + FACE_ROWS, :] = joined[rows_of(tab[t.slot + f]), :].astype(F32)
+    dirn[order:, :] = grad_all[...] - shift[order:, :]
     gather(dirn, zfull, tab, faces)
     curv = jnp.zeros((1, columns), F32)
     for band, product in apply(made, dual, moved, zfull, faces):

time: 134 us -> 134 us (level)
  no operation moved by 1% of the time
where the time goes in v3:
time: 134 us
  starting transfers between devices  54.3 us (41%)
  blocking collectives  27.9 us (21%)
  waiting for transfers between devices  27 us (20%)
  Pallas kernels  24.1 us (18%)
    ppermute x18, starting transfers between devices, swap_all(): lax.ppermute(send, 'sub', swap_pairs(m, count))  30.7 us
    all_to_all x3, blocking collectives, exchange(): return lax.all_to_all(value, ('sub', 'grp'), 0, 0)  27.9 us
    pallas_call x14, Pallas kernels, call(): pl.pallas_call(kernel, name=name, out_shape=[(HBM if space == HBM else ja...  24.1 us
    ppermute x18, waiting for transfers between devices, swap_all(): lax.ppermute(send, 'sub', swap_pairs(m, count))  9.96 us
    all_to_all x3, starting transfers between devices, exchange(): return lax.all_to_all(value, ('sub', 'grp'), 0, 0)  9.48 us
    ppermute x4, starting transfers between devices, swap_direct(): lax.ppermute(send, 'sub', swap_pairs(m, count))  7.25 us
    ppermute x6, waiting for transfers between devices, swap_all(): lax.ppermute(passed, 'sub', swap_pairs(3, count))  7.06 us
    all_to_all x3, waiting for transfers between devices, exchange(): return lax.all_to_all(value, ('sub', 'grp'), 0, 0)  6.83 us
  transfers between devices with their start and end apart: 34, of which 15 were waited for; matrix products, arithmetic and copies ran while one was open for 0% of the time, Pallas kernels for 6%

profile of v3, /device:TPU:0, one launch (start us, length us, event | category | flops | bytes accessed | tf_op | source)
XLA Modules:
  0.0 133.7 jit_solution(11334398596715175902)
XLA Ops:
  0.0 2.3 %start.1 = (s32[128]{0:T(128)S(1)}, bf16[16,1024]{1,0:T(8,128)(2,1)S(1)}, bf16[1024,128]{1,0:T(8,128)(2,1)S(1)}, bf16[32,128]{1,0:T(8,128)(2,1)S(1)}, bf16[320,1...) custom-call(s32[128]{0:T(128)S(1)} %compare_select_fusion.1.pos_v, ...), custom_call_target="tpu_custom_call" | custom-call | tf_op jit(solution)/shard_map/start/pallas_call | solution.py:467
  2.3 3.1 %collective-permute-start = (bf16[320,128]{1,0:T(8,128)(2,1)S(1)}, bf16[320,128]{1,0:T(8,128)(2,1)S(1)}, u32[]{:S(2)}, u32[]{:S(2)}) collective-permute-start(bf16[320,128]{1,0:T(8,128)(2,1)S(1)} %get-tuple-element.70), channel_id=1, source_target_pairs={{0,8},{8,0},{4,12},{12,4},{16,24},{24,16},{20,28},{28,20},{1,9},{9... | collective-permute-start | bytes 245768 | tf_op jit(solution)/shard_map/ppermute | solution.py:55
  6.7 2.8 %collective-permute-start.3 = (bf16[320,128]{1,0:T(8,128)(2,1)S(1)}, bf16[320,128]{1,0:T(8,128)(2,1)S(1)}, u32[]{:S(2)}, u32[]{:S(2)}) collective-permute-start(bf16[320,128]{1,0:T(8,128)(2,1)S(1)} %get-tuple-element.73), channel_id=1, source_target_pairs={{0,4},{4,0},{8,12},{12,8},{16,20},{20,16},{24,28},{28,24},{1,5},{5... | collective-permute-start | bytes 245768 | tf_op jit(solution)/shard_map/ppermute | solution.py:55
  9.6 3.2 %collective-permute-done.3.rest_3_ = bf16[320,128]{1,0:T(8,128)(2,1)S(1)} collective-permute-done((bf16[320,128]{1,0:T(8,128)(2,1)S(1)}, bf16[320,128]{1,0:T(8,128)(2,1)S(1)}, u32[]{:S(2)}, u32[]{:S(2)}) %collective-permute-start.3) | collective-permute-done | bytes 81952 | tf_op jit(solution)/shard_map/ppermute | solution.py:55
  14.9 7.3 %collective-permute-start.8 = (bf16[256,128]{1,0:T(8,128)(2,1)S(1)}, bf16[256,128]{1,0:T(8,128)(2,1)S(1)}, u32[]{:S(2)}, u32[]{:S(2)}) collective-permute-start(bf16[256,128]{1,0:T(8,128)(2,1)S(1)} %get-tuple-element.86), channel_id=1, source_target_pairs={{0,8},{8,0},{4,12},{12,4},{16,24},{24,16},{20,28},{28,20},{1,9},{9... | collective-permute-start | bytes 196616 | tf_op jit(solution)/shard_map/ppermute | solution.py:62
  29.1 2.5 %inner.3 = (f32[768,128]{1,0:T(8,128)S(1)}, f32[8,128]{1,0:T(8,128)S(1)}) custom-call(bf16[1,1024,1024]{2,1,0:T(8,128)(2,1)} %dual_h.13, f32[1024,128]{1,0:T(8,128)} %loads_h.7, bf16[1024,128]{1,0:T(8,128)(2,1)S(1)} %get-tuple-element.79.zfull, bf16[16,1024]{1,0:T(8,128)(2,1)S(1)} %get-tuple-element.78.rows), custom_call_target="tpu_custom_call" | custom-call | flops 201326592 | bytes 1572864 | tf_op jit(solution)/shard_map/inner/pallas_call | solution.py:467
  32.7 2.1 %collective-permute-start.11 = (bf16[256,128]{1,0:T(8,128)(2,1)S(1)}, bf16[256,128]{1,0:T(8,128)(2,1)S(1)}, u32[]{:S(2)}, u32[]{:S(2)}) collective-permute-start(bf16[256,128]{1,0:T(8,128)(2,1)S(1)} %get-tuple-element.88), channel_id=1, source_target_pairs={{0,8},{8,0},{4,12},{12,4},{16,24},{24,16},{20,28},{28,20},{1,9},{9... | collective-permute-start | bytes 196616 | tf_op jit(solution)/shard_map/ppermute | solution.py:62
  35.5 3.1 %all-to-all-start = ((f32[32,8,128]{2,1,0:T(8,128)}), f32[32,8,128]{2,1,0:T(8,128)S(1)}, u32[]{:S(2)}, u32[]{:S(2)}) async-start(f32[32,8,128]{2,1,0:T(8,128)} %get-tuple-element.91), calls=%async_computation | async-start | bytes 262144 | tf_op jit(solution)/shard_map/all_to_all | solution.py:495
  38.6 1.8 %collective-permute-start.14 = (bf16[128,128]{1,0:T(8,128)(2,1)S(1)}, bf16[128,128]{1,0:T(8,128)(2,1)S(1)}, u32[]{:S(2)}, u32[]{:S(2)}) collective-permute-start(bf16[128,128]{1,0:T(8,128)(2,1)S(1)} %get-tuple-element.94), channel_id=1, source_target_pairs={{0,4},{4,0},{8,12},{12,8},{16,20},{20,16},{24,28},{28,24},{1,5},{5... | collective-permute-start | bytes 98312 | tf_op jit(solution)/shard_map/ppermute | solution.py:62
  40.8 2.0 %collective-permute-done.14.rest_2_ = bf16[128,128]{1,0:T(8,128)(2,1)S(1)} collective-permute-done((bf16[128,128]{1,0:T(8,128)(2,1)S(1)}, bf16[128,128]{1,0:T(8,128)(2,1)S(1)}, u32[]{:S(2)}, u32[]{:S(2)}) %collective-permute-start.14) | collective-permute-done | bytes 32800 | tf_op jit(solution)/shard_map/ppermute | solution.py:62
  42.8 1.8 %collective-permute-done.13.rest_1_ = bf16[128,128]{1,0:T(8,128)(2,1)S(1)} collective-permute-done((bf16[128,128]{1,0:T(8,128)(2,1)S(1)}, bf16[128,128]{1,0:T(8,128)(2,1)S(1)}, u32[]{:S(2)}, u32[]{:S(2)}) %collective-permute-start.13) | collective-permute-done | bytes 32800 | tf_op jit(solution)/shard_map/ppermute | solution.py:65
  44.6 2.3 %all-to-all-done.every = f32[32,8,128]{2,1,0:T(8,128)S(1)} async-done(((f32[32,8,128]{2,1,0:T(8,128)}), f32[32,8,128]{2,1,0:T(8,128)S(1)}, u32[]{:S(2)}, u32[]{:S(2)}) %all-to-all-start) | async-done | bytes 131104 | tf_op jit(solution)/shard_map/all_to_all | solution.py:495
  46.8 2.2 %direction.3 = (f32[1280,128]{1,0:T(8,128)S(1)}, f32[32,2,128]{2,1,0:T(2,128)S(1)}) custom-call(s32[128]{0:T(128)S(1)} %get-tuple-element.67.tab_v, bf16[1,1024,1024]{2,1,0:T(8,128)(2,1)} %dual_h.13, bf16[256,1024]{1,0:T(8,128)(2,1)S(1)} %get-tuple-element.74.dual, bf16[256,128]{1,0:T(8,128)(2,1)S(1)} %collective-permute-done.11.near, ...), custom_call_target="tpu_custom_call" | custom-call | tf_op jit(solution)/shard_map/direction/pallas_call | solution.py:467
  49.1 9.3 %all_to_all.30.parts = f32[32,2,128]{2,1,0:T(2,128)S(1)} all-to-all(f32[32,2,128]{2,1,0:T(2,128)S(1)} %get-tuple-element.96), channel_id=1, replica_groups=mesh['sub'=8,'grp'=4] {'sub','grp'}, dimensions={0} | all-to-all | bytes 65536 | tf_op jit(solution)/shard_map/all_to_all | solution.py:495
  60.1 2.5 %collective-permute-start.16 = (bf16[256,128]{1,0:T(8,128)(2,1)S(1)}, bf16[256,128]{1,0:T(8,128)(2,1)S(1)}, u32[]{:S(2)}, u32[]{:S(2)}) collective-permute-start(bf16[256,128]{1,0:T(8,128)(2,1)S(1)} %get-tuple-element.103), channel_id=1, source_target_pairs={{0,8},{8,0},{4,12},{12,4},{16,24},{24,16},{20,28},{28,20},{1,9},{9... | collective-permute-start | bytes 196616 | tf_op jit(solution)/shard_map/ppermute | solution.py:62
  65.5 2.5 %inner.4 = (f32[768,128]{1,0:T(8,128)S(1)}, f32[8,128]{1,0:T(8,128)S(1)}) custom-call(bf16[1,1024,1024]{2,1,0:T(8,128)(2,1)} %dual_h.13, f32[1024,128]{1,0:T(8,128)} %loads_h.7, bf16[1024,128]{1,0:T(8,128)(2,1)S(1)} %get-tuple-element.100.zfull, bf16[16,1024]{1,0:T(8,128)(2,1)S(1)} %get-tuple-element.78.rows), custom_call_target="tpu_custom_call" | custom-call | flops 201326592 | bytes 1572864 | tf_op jit(solution)/shard_map/inner/pallas_call | solution.py:467
  69.8 2.1 %collective-permute-start.19 = (bf16[256,128]{1,0:T(8,128)(2,1)S(1)}, bf16[256,128]{1,0:T(8,128)(2,1)S(1)}, u32[]{:S(2)}, u32[]{:S(2)}) collective-permute-start(bf16[256,128]{1,0:T(8,128)(2,1)S(1)} %get-tuple-element.105), channel_id=1, source_target_pairs={{0,8},{8,0},{4,12},{12,4},{16,24},{24,16},{20,28},{28,20},{1,9},{9... | collective-permute-start | bytes 196616 | tf_op jit(solution)/shard_map/ppermute | solution.py:62
  72.6 3.2 %all-to-all-start.2 = ((f32[32,8,128]{2,1,0:T(8,128)}), f32[32,8,128]{2,1,0:T(8,128)S(1)}, u32[]{:S(2)}, u32[]{:S(2)}) async-start(f32[32,8,128]{2,1,0:T(8,128)} %get-tuple-element.108), calls=%async_computation.2 | async-start | bytes 262144 | tf_op jit(solution)/shard_map/all_to_all | solution.py:495
  75.8 1.8 %collective-permute-start.22 = (bf16[128,128]{1,0:T(8,128)(2,1)S(1)}, bf16[128,128]{1,0:T(8,128)(2,1)S(1)}, u32[]{:S(2)}, u32[]{:S(2)}) collective-permute-start(bf16[128,128]{1,0:T(8,128)(2,1)S(1)} %get-tuple-element.110), channel_id=1, source_target_pairs={{0,4},{4,0},{8,12},{12,8},{16,20},{20,16},{24,28},{28,24},{1,5},{5... | collective-permute-start | bytes 98312 | tf_op jit(solution)/shard_map/ppermute | solution.py:62
  78.0 2.0 %collective-permute-done.22.rest_2_ = bf16[128,128]{1,0:T(8,128)(2,1)S(1)} collective-permute-done((bf16[128,128]{1,0:T(8,128)(2,1)S(1)}, bf16[128,128]{1,0:T(8,128)(2,1)S(1)}, u32[]{:S(2)}, u32[]{:S(2)}) %collective-permute-start.22) | collective-permute-done | bytes 32800 | tf_op jit(solution)/shard_map/ppermute | solution.py:62
  81.7 2.3 %all-to-all-done.2.every = f32[32,8,128]{2,1,0:T(8,128)S(1)} async-done(((f32[32,8,128]{2,1,0:T(8,128)}), f32[32,8,128]{2,1,0:T(8,128)S(1)}, u32[]{:S(2)}, u32[]{:S(2)}) %all-to-all-start.2) | async-done | bytes 131104 | tf_op jit(solution)/shard_map/all_to_all | solution.py:495
  84.0 2.2 %direction.4 = (f32[1280,128]{1,0:T(8,128)S(1)}, f32[32,2,128]{2,1,0:T(2,128)S(1)}) custom-call(s32[128]{0:T(128)S(1)} %get-tuple-element.67.tab_v, bf16[1,1024,1024]{2,1,0:T(8,128)(2,1)} %dual_h.13, bf16[256,1024]{1,0:T(8,128)(2,1)S(1)} %get-tuple-element.74.dual, bf16[256,128]{1,0:T(8,128)(2,1)S(1)} %collective-permute-done.19.near, ...), custom_call_target="tpu_custom_call" | custom-call | tf_op jit(solution)/shard_map/direction/pallas_call | solution.py:467
  86.2 9.3 %all_to_all.31.parts = f32[32,2,128]{2,1,0:T(2,128)S(1)} all-to-all(f32[32,2,128]{2,1,0:T(2,128)S(1)} %get-tuple-element.111), channel_id=1, replica_groups=mesh['sub'=8,'grp'=4] {'sub','grp'}, dimensions={0} | all-to-all | bytes 65536 | tf_op jit(solution)/shard_map/all_to_all | solution.py:495
  97.3 2.5 %collective-permute-start.24 = (bf16[256,128]{1,0:T(8,128)(2,1)S(1)}, bf16[256,128]{1,0:T(8,128)(2,1)S(1)}, u32[]{:S(2)}, u32[]{:S(2)}) collective-permute-start(bf16[256,128]{1,0:T(8,128)(2,1)S(1)} %get-tuple-element.118), channel_id=1, source_target_pairs={{0,8},{8,0},{4,12},{12,4},{16,24},{24,16},{20,28},{28,20},{1,9},{9... | collective-permute-start | bytes 196616 | tf_op jit(solution)/shard_map/ppermute | solution.py:62
  102.6 2.5 %inner.5 = (f32[768,128]{1,0:T(8,128)S(1)}, f32[8,128]{1,0:T(8,128)S(1)}) custom-call(bf16[1,1024,1024]{2,1,0:T(8,128)(2,1)} %dual_h.13, f32[1024,128]{1,0:T(8,128)} %loads_h.7, bf16[1024,128]{1,0:T(8,128)(2,1)S(1)} %get-tuple-element.115.zfull, bf16[16,1024]{1,0:T(8,128)(2,1)S(1)} %get-tuple-element.78.rows), custom_call_target="tpu_custom_call" | custom-call | flops 201326592 | bytes 1572864 | tf_op jit(solution)/shard_map/inner/pallas_call | solution.py:467
  107.0 2.1 %collective-permute-start.27 = (bf16[256,128]{1,0:T(8,128)(2,1)S(1)}, bf16[256,128]{1,0:T(8,128)(2,1)S(1)}, u32[]{:S(2)}, u32[]{:S(2)}) collective-permute-start(bf16[256,128]{1,0:T(8,128)(2,1)S(1)} %get-tuple-element.120), channel_id=1, source_target_pairs={{0,8},{8,0},{4,12},{12,4},{16,24},{24,16},{20,28},{28,20},{1,9},{9... | collective-permute-start | bytes 196616 | tf_op jit(solution)/shard_map/ppermute | solution.py:62
  109.8 3.2 %all-to-all-start.4 = ((f32[32,8,128]{2,1,0:T(8,128)}), f32[32,8,128]{2,1,0:T(8,128)S(1)}, u32[]{:S(2)}, u32[]{:S(2)}) async-start(f32[32,8,128]{2,1,0:T(8,128)} %get-tuple-element.123), calls=%async_computation.4 | async-start | bytes 262144 | tf_op jit(solution)/shard_map/all_to_all | solution.py:495
  113.0 1.8 %collective-permute-start.30 = (bf16[128,128]{1,0:T(8,128)(2,1)S(1)}, bf16[128,128]{1,0:T(8,128)(2,1)S(1)}, u32[]{:S(2)}, u32[]{:S(2)}) collective-permute-start(bf16[128,128]{1,0:T(8,128)(2,1)S(1)} %get-tuple-element.125), channel_id=1, source_target_pairs={{0,4},{4,0},{8,12},{12,8},{16,20},{20,16},{24,28},{28,24},{1,5},{5... | collective-permute-start | bytes 98312 | tf_op jit(solution)/shard_map/ppermute | solution.py:62
  115.1 2.0 %collective-permute-done.30.rest_2_ = bf16[128,128]{1,0:T(8,128)(2,1)S(1)} collective-permute-done((bf16[128,128]{1,0:T(8,128)(2,1)S(1)}, bf16[128,128]{1,0:T(8,128)(2,1)S(1)}, u32[]{:S(2)}, u32[]{:S(2)}) %collective-permute-start.30) | collective-permute-done | bytes 32800 | tf_op jit(solution)/shard_map/ppermute | solution.py:62
  118.9 2.3 %all-to-all-done.4.every = f32[32,8,128]{2,1,0:T(8,128)S(1)} async-done(((f32[32,8,128]{2,1,0:T(8,128)}), f32[32,8,128]{2,1,0:T(8,128)S(1)}, u32[]{:S(2)}, u32[]{:S(2)}) %all-to-all-start.4) | async-done | bytes 131104 | tf_op jit(solution)/shard_map/all_to_all | solution.py:495
  121.2 2.2 %direction.5 = (f32[1280,128]{1,0:T(8,128)S(1)}, f32[32,2,128]{2,1,0:T(2,128)S(1)}) custom-call(s32[128]{0:T(128)S(1)} %get-tuple-element.67.tab_v, bf16[1,1024,1024]{2,1,0:T(8,128)(2,1)} %dual_h.13, bf16[256,1024]{1,0:T(8,128)(2,1)S(1)} %get-tuple-element.74.dual, bf16[256,128]{1,0:T(8,128)(2,1)S(1)} %collective-permute-done.27.near, ...), custom_call_target="tpu_custom_call" | custom-call | tf_op jit(solution)/shard_map/direction/pallas_call | solution.py:467
  123.4 9.3 %all_to_all.32.parts = f32[32,2,128]{2,1,0:T(2,128)S(1)} all-to-all(f32[32,2,128]{2,1,0:T(2,128)S(1)} %get-tuple-element.126), channel_id=1, replica_groups=mesh['sub'=8,'grp'=4] {'sub','grp'}, dimensions={0} | all-to-all | bytes 65536 | tf_op jit(solution)/shard_map/all_to_all | solution.py:495
  (60 shorter events, 31.8 us)
Async XLA Ops:
  2.3 7.3 %collective-permute-start = (bf16[320,128]{1,0:T(8,128)(2,1)S(1)}, bf16[320,128]{1,0:T(8,128)(2,1)S(1)}, u32[]{:S(2)}, u32[]{:S(2)}) collective-permute-start(bf16[320,128]{1,0:T(8,128)(2,1)S(1)} %get-tuple-element.70), channel_id=1, source_target_pairs={{0,8},{8,0},{4,12},{12,4},{16,24},{24,16},{20,28},{28,20},{1,9},{9... | collective-permute-start | bytes 245768 | tf_op jit(solution)/shard_map/ppermute | solution.py:55
  5.4 4.2 %collective-permute-start.1 = (bf16[320,128]{1,0:T(8,128)(2,1)S(1)}, bf16[320,128]{1,0:T(8,128)(2,1)S(1)}, u32[]{:S(2)}, u32[]{:S(2)}) collective-permute-start(bf16[320,128]{1,0:T(8,128)(2,1)S(1)} %get-tuple-element.71), channel_id=1, source_target_pairs={{4,8},{8,4},{12,16},{16,12},{20,24},{24,20},{5,9},{9,5},{13,17},{1... | collective-permute-start | bytes 245768 | tf_op jit(solution)/shard_map/ppermute | solution.py:55
  6.7 6.0 %collective-permute-start.3 = (bf16[320,128]{1,0:T(8,128)(2,1)S(1)}, bf16[320,128]{1,0:T(8,128)(2,1)S(1)}, u32[]{:S(2)}, u32[]{:S(2)}) collective-permute-start(bf16[320,128]{1,0:T(8,128)(2,1)S(1)} %get-tuple-element.73), channel_id=1, source_target_pairs={{0,4},{4,0},{8,12},{12,8},{16,20},{20,16},{24,28},{28,24},{1,5},{5... | collective-permute-start | bytes 245768 | tf_op jit(solution)/shard_map/ppermute | solution.py:55
  14.3 9.6 %collective-permute-start.7 = (bf16[256,128]{1,0:T(8,128)(2,1)S(1)}, bf16[256,128]{1,0:T(8,128)(2,1)S(1)}, u32[]{:S(2)}, u32[]{:S(2)}) collective-permute-start(bf16[256,128]{1,0:T(8,128)(2,1)S(1)} %get-tuple-element.85), channel_id=1, source_target_pairs={{8,16},{16,8},{12,20},{20,12},{9,17},{17,9},{13,21},{21,13},{10,18... | collective-permute-start | bytes 196616 | tf_op jit(solution)/shard_map/ppermute | solution.py:62
  14.9 9.5 %collective-permute-start.8 = (bf16[256,128]{1,0:T(8,128)(2,1)S(1)}, bf16[256,128]{1,0:T(8,128)(2,1)S(1)}, u32[]{:S(2)}, u32[]{:S(2)}) collective-permute-start(bf16[256,128]{1,0:T(8,128)(2,1)S(1)} %get-tuple-element.86), channel_id=1, source_target_pairs={{0,8},{8,0},{4,12},{12,4},{16,24},{24,16},{20,28},{28,20},{1,9},{9... | collective-permute-start | bytes 196616 | tf_op jit(solution)/shard_map/ppermute | solution.py:62
  22.2 9.5 %collective-permute-start.10 = (bf16[128,128]{1,0:T(8,128)(2,1)S(1)}, bf16[128,128]{1,0:T(8,128)(2,1)S(1)}, u32[]{:S(2)}, u32[]{:S(2)}) collective-permute-start(bf16[128,128]{1,0:T(8,128)(2,1)S(1)} %get-tuple-element.87), channel_id=1, source_target_pairs={{0,4},{4,0},{8,12},{12,8},{16,20},{20,16},{24,28},{28,24},{1,5},{5... | collective-permute-start | bytes 98312 | tf_op jit(solution)/shard_map/ppermute | solution.py:62
  24.5 7.2 %collective-permute-start.9 = (bf16[128,128]{1,0:T(8,128)(2,1)S(1)}, bf16[128,128]{1,0:T(8,128)(2,1)S(1)}, u32[]{:S(2)}, u32[]{:S(2)}) collective-permute-start(bf16[128,128]{1,0:T(8,128)(2,1)S(1)} %slice_select_fusion.5), channel_id=1, source_target_pairs={{0,4},{4,0},{8,12},{12,8},{16,20},{20,16},{24,28},{28,24},{1,5},{5... | collective-permute-start | bytes 98312 | tf_op jit(solution)/shard_map/ppermute | solution.py:65
  26.2 5.5 %collective-permute-start.4 = (bf16[48,128]{1,0:T(8,128)(2,1)S(1)}, bf16[48,128]{1,0:T(8,128)(2,1)S(1)}, u32[]{:S(2)}, u32[]{:S(2)}) collective-permute-start(bf16[48,128]{1,0:T(8,128)(2,1)S(1)} %get-tuple-element.82), channel_id=1, source_target_pairs={{0,1},{1,2},{2,3},{3,0},{4,5},{5,6},{6,7},{7,4},{8,9},{9,10},{10,1... | collective-permute-start | bytes 36872 | tf_op jit(solution)/shard_map/ppermute | solution.py:491
  26.2 5.5 %collective-permute-start.5 = (bf16[48,128]{1,0:T(8,128)(2,1)S(1)}, bf16[48,128]{1,0:T(8,128)(2,1)S(1)}, u32[]{:S(2)}, u32[]{:S(2)}) collective-permute-start(bf16[48,128]{1,0:T(8,128)(2,1)S(1)} %get-tuple-element.83), channel_id=1, source_target_pairs={{0,2},{1,3},{2,0},{3,1},{4,6},{5,7},{6,4},{7,5},{8,10},{9,11},{10,... | collective-permute-start | bytes 36872 | tf_op jit(solution)/shard_map/ppermute | solution.py:491
  27.7 4.0 %collective-permute-start.6 = (bf16[48,128]{1,0:T(8,128)(2,1)S(1)}, bf16[48,128]{1,0:T(8,128)(2,1)S(1)}, u32[]{:S(2)}, u32[]{:S(2)}) collective-permute-start(bf16[48,128]{1,0:T(8,128)(2,1)S(1)} %get-tuple-element.84), channel_id=1, source_target_pairs={{0,3},{1,0},{2,1},{3,2},{4,7},{5,4},{6,5},{7,6},{8,11},{9,8},{10,9... | collective-permute-start | bytes 36872 | tf_op jit(solution)/shard_map/ppermute | solution.py:491
  32.7 7.7 %collective-permute-start.11 = (bf16[256,128]{1,0:T(8,128)(2,1)S(1)}, bf16[256,128]{1,0:T(8,128)(2,1)S(1)}, u32[]{:S(2)}, u32[]{:S(2)}) collective-permute-start(bf16[256,128]{1,0:T(8,128)(2,1)S(1)} %get-tuple-element.88), channel_id=1, source_target_pairs={{0,8},{8,0},{4,12},{12,4},{16,24},{24,16},{20,28},{28,20},{1,9},{9... | collective-permute-start | bytes 196616 | tf_op jit(solution)/shard_map/ppermute | solution.py:62
  34.8 5.6 %collective-permute-start.12 = (bf16[256,128]{1,0:T(8,128)(2,1)S(1)}, bf16[256,128]{1,0:T(8,128)(2,1)S(1)}, u32[]{:S(2)}, u32[]{:S(2)}) collective-permute-start(bf16[256,128]{1,0:T(8,128)(2,1)S(1)} %get-tuple-element.93), channel_id=1, source_target_pairs={{8,16},{16,8},{12,20},{20,12},{9,17},{17,9},{13,21},{21,13},{10,18... | collective-permute-start | bytes 196616 | tf_op jit(solution)/shard_map/ppermute | solution.py:62
  35.5 11.3 %all-to-all-start = ((f32[32,8,128]{2,1,0:T(8,128)}), f32[32,8,128]{2,1,0:T(8,128)S(1)}, u32[]{:S(2)}, u32[]{:S(2)}) async-start(f32[32,8,128]{2,1,0:T(8,128)} %get-tuple-element.91), calls=%async_computation | async-start | bytes 262144 | tf_op jit(solution)/shard_map/all_to_all | solution.py:495
  38.6 4.2 %collective-permute-start.14 = (bf16[128,128]{1,0:T(8,128)(2,1)S(1)}, bf16[128,128]{1,0:T(8,128)(2,1)S(1)}, u32[]{:S(2)}, u32[]{:S(2)}) collective-permute-start(bf16[128,128]{1,0:T(8,128)(2,1)S(1)} %get-tuple-element.94), channel_id=1, source_target_pairs={{0,4},{4,0},{8,12},{12,8},{16,20},{20,16},{24,28},{28,24},{1,5},{5... | collective-permute-start | bytes 98312 | tf_op jit(solution)/shard_map/ppermute | solution.py:62
  40.5 4.1 %collective-permute-start.13 = (bf16[128,128]{1,0:T(8,128)(2,1)S(1)}, bf16[128,128]{1,0:T(8,128)(2,1)S(1)}, u32[]{:S(2)}, u32[]{:S(2)}) collective-permute-start(bf16[128,128]{1,0:T(8,128)(2,1)S(1)} %slice_select_fusion.4), channel_id=1, source_target_pairs={{0,4},{4,0},{8,12},{12,8},{16,20},{20,16},{24,28},{28,24},{1,5},{5... | collective-permute-start | bytes 98312 | tf_op jit(solution)/shard_map/ppermute | solution.py:65
  59.4 3.7 %collective-permute-start.15 = (bf16[256,128]{1,0:T(8,128)(2,1)S(1)}, bf16[256,128]{1,0:T(8,128)(2,1)S(1)}, u32[]{:S(2)}, u32[]{:S(2)}) collective-permute-start(bf16[256,128]{1,0:T(8,128)(2,1)S(1)} %get-tuple-element.102), channel_id=1, source_target_pairs={{8,16},{16,8},{12,20},{20,12},{9,17},{17,9},{13,21},{21,13},{10,18... | collective-permute-start | bytes 196616 | tf_op jit(solution)/shard_map/ppermute | solution.py:62
  60.1 4.7 %collective-permute-start.16 = (bf16[256,128]{1,0:T(8,128)(2,1)S(1)}, bf16[256,128]{1,0:T(8,128)(2,1)S(1)}, u32[]{:S(2)}, u32[]{:S(2)}) collective-permute-start(bf16[256,128]{1,0:T(8,128)(2,1)S(1)} %get-tuple-element.103), channel_id=1, source_target_pairs={{0,8},{8,0},{4,12},{12,4},{16,24},{24,16},{20,28},{28,20},{1,9},{9... | collective-permute-start | bytes 196616 | tf_op jit(solution)/shard_map/ppermute | solution.py:62
  62.6 5.4 %collective-permute-start.18 = (bf16[128,128]{1,0:T(8,128)(2,1)S(1)}, bf16[128,128]{1,0:T(8,128)(2,1)S(1)}, u32[]{:S(2)}, u32[]{:S(2)}) collective-permute-start(bf16[128,128]{1,0:T(8,128)(2,1)S(1)} %get-tuple-element.104), channel_id=1, source_target_pairs={{0,4},{4,0},{8,12},{12,8},{16,20},{20,16},{24,28},{28,24},{1,5},{5... | collective-permute-start | bytes 98312 | tf_op jit(solution)/shard_map/ppermute | solution.py:62
  64.8 4.0 %collective-permute-start.17 = (bf16[128,128]{1,0:T(8,128)(2,1)S(1)}, bf16[128,128]{1,0:T(8,128)(2,1)S(1)}, u32[]{:S(2)}, u32[]{:S(2)}) collective-permute-start(bf16[128,128]{1,0:T(8,128)(2,1)S(1)} %slice_select_fusion.3), channel_id=1, source_target_pairs={{0,4},{4,0},{8,12},{12,8},{16,20},{20,16},{24,28},{28,24},{1,5},{5... | collective-permute-start | bytes 98312 | tf_op jit(solution)/shard_map/ppermute | solution.py:65
  69.8 7.8 %collective-permute-start.19 = (bf16[256,128]{1,0:T(8,128)(2,1)S(1)}, bf16[256,128]{1,0:T(8,128)(2,1)S(1)}, u32[]{:S(2)}, u32[]{:S(2)}) collective-permute-start(bf16[256,128]{1,0:T(8,128)(2,1)S(1)} %get-tuple-element.105), channel_id=1, source_target_pairs={{0,8},{8,0},{4,12},{12,4},{16,24},{24,16},{20,28},{28,20},{1,9},{9... | collective-permute-start | bytes 196616 | tf_op jit(solution)/shard_map/ppermute | solution.py:62
  71.9 5.7 %collective-permute-start.20 = (bf16[256,128]{1,0:T(8,128)(2,1)S(1)}, bf16[256,128]{1,0:T(8,128)(2,1)S(1)}, u32[]{:S(2)}, u32[]{:S(2)}) collective-permute-start(bf16[256,128]{1,0:T(8,128)(2,1)S(1)} %get-tuple-element.109), channel_id=1, source_target_pairs={{8,16},{16,8},{12,20},{20,12},{9,17},{17,9},{13,21},{21,13},{10,18... | collective-permute-start | bytes 196616 | tf_op jit(solution)/shard_map/ppermute | solution.py:62
  72.6 11.4 %all-to-all-start.2 = ((f32[32,8,128]{2,1,0:T(8,128)}), f32[32,8,128]{2,1,0:T(8,128)S(1)}, u32[]{:S(2)}, u32[]{:S(2)}) async-start(f32[32,8,128]{2,1,0:T(8,128)} %get-tuple-element.108), calls=%async_computation.2 | async-start | bytes 262144 | tf_op jit(solution)/shard_map/all_to_all | solution.py:495
  75.8 4.2 %collective-permute-start.22 = (bf16[128,128]{1,0:T(8,128)(2,1)S(1)}, bf16[128,128]{1,0:T(8,128)(2,1)S(1)}, u32[]{:S(2)}, u32[]{:S(2)}) collective-permute-start(bf16[128,128]{1,0:T(8,128)(2,1)S(1)} %get-tuple-element.110), channel_id=1, source_target_pairs={{0,4},{4,0},{8,12},{12,8},{16,20},{20,16},{24,28},{28,24},{1,5},{5... | collective-permute-start | bytes 98312 | tf_op jit(solution)/shard_map/ppermute | solution.py:62
  77.6 4.1 %collective-permute-start.21 = (bf16[128,128]{1,0:T(8,128)(2,1)S(1)}, bf16[128,128]{1,0:T(8,128)(2,1)S(1)}, u32[]{:S(2)}, u32[]{:S(2)}) collective-permute-start(bf16[128,128]{1,0:T(8,128)(2,1)S(1)} %slice_select_fusion.2), channel_id=1, source_target_pairs={{0,4},{4,0},{8,12},{12,8},{16,20},{20,16},{24,28},{28,24},{1,5},{5... | collective-permute-start | bytes 98312 | tf_op jit(solution)/shard_map/ppermute | solution.py:65
  97.3 4.7 %collective-permute-start.24 = (bf16[256,128]{1,0:T(8,128)(2,1)S(1)}, bf16[256,128]{1,0:T(8,128)(2,1)S(1)}, u32[]{:S(2)}, u32[]{:S(2)}) collective-permute-start(bf16[256,128]{1,0:T(8,128)(2,1)S(1)} %get-tuple-element.118), channel_id=1, source_target_pairs={{0,8},{8,0},{4,12},{12,4},{16,24},{24,16},{20,28},{28,20},{1,9},{9... | collective-permute-start | bytes 196616 | tf_op jit(solution)/shard_map/ppermute | solution.py:62
  99.8 5.4 %collective-permute-start.26 = (bf16[128,128]{1,0:T(8,128)(2,1)S(1)}, bf16[128,128]{1,0:T(8,128)(2,1)S(1)}, u32[]{:S(2)}, u32[]{:S(2)}) collective-permute-start(bf16[128,128]{1,0:T(8,128)(2,1)S(1)} %get-tuple-element.119), channel_id=1, source_target_pairs={{0,4},{4,0},{8,12},{12,8},{16,20},{20,16},{24,28},{28,24},{1,5},{5... | collective-permute-start | bytes 98312 | tf_op jit(solution)/shard_map/ppermute | solution.py:62
  102.0 4.0 %collective-permute-start.25 = (bf16[128,128]{1,0:T(8,128)(2,1)S(1)}, bf16[128,128]{1,0:T(8,128)(2,1)S(1)}, u32[]{:S(2)}, u32[]{:S(2)}) collective-permute-start(bf16[128,128]{1,0:T(8,128)(2,1)S(1)} %slice_select_fusion.1), channel_id=1, source_target_pairs={{0,4},{4,0},{8,12},{12,8},{16,20},{20,16},{24,28},{28,24},{1,5},{5... | collective-permute-start | bytes 98312 | tf_op jit(solution)/shard_map/ppermute | solution.py:65
  107.0 7.8 %collective-permute-start.27 = (bf16[256,128]{1,0:T(8,128)(2,1)S(1)}, bf16[256,128]{1,0:T(8,128)(2,1)S(1)}, u32[]{:S(2)}, u32[]{:S(2)}) collective-permute-start(bf16[256,128]{1,0:T(8,128)(2,1)S(1)} %get-tuple-element.120), channel_id=1, source_target_pairs={{0,8},{8,0},{4,12},{12,4},{16,24},{24,16},{20,28},{28,20},{1,9},{9... | collective-permute-start | bytes 196616 | tf_op jit(solution)/shard_map/ppermute | solution.py:62
  109.1 5.7 %collective-permute-start.28 = (bf16[256,128]{1,0:T(8,128)(2,1)S(1)}, bf16[256,128]{1,0:T(8,128)(2,1)S(1)}, u32[]{:S(2)}, u32[]{:S(2)}) collective-permute-start(bf16[256,128]{1,0:T(8,128)(2,1)S(1)} %get-tuple-element.124), channel_id=1, source_target_pairs={{8,16},{16,8},{12,20},{20,12},{9,17},{17,9},{13,21},{21,13},{10,18... | collective-permute-start | bytes 196616 | tf_op jit(solution)/shard_map/ppermute | solution.py:62
  109.8 11.4 %all-to-all-start.4 = ((f32[32,8,128]{2,1,0:T(8,128)}), f32[32,8,128]{2,1,0:T(8,128)S(1)}, u32[]{:S(2)}, u32[]{:S(2)}) async-start(f32[32,8,128]{2,1,0:T(8,128)} %get-tuple-element.123), calls=%async_computation.4 | async-start | bytes 262144 | tf_op jit(solution)/shard_map/all_to_all | solution.py:495
  113.0 4.2 %collective-permute-start.30 = (bf16[128,128]{1,0:T(8,128)(2,1)S(1)}, bf16[128,128]{1,0:T(8,128)(2,1)S(1)}, u32[]{:S(2)}, u32[]{:S(2)}) collective-permute-start(bf16[128,128]{1,0:T(8,128)(2,1)S(1)} %get-tuple-element.125), channel_id=1, source_target_pairs={{0,4},{4,0},{8,12},{12,8},{16,20},{20,16},{24,28},{28,24},{1,5},{5... | collective-permute-start | bytes 98312 | tf_op jit(solution)/shard_map/ppermute | solution.py:62
  114.8 4.1 %collective-permute-start.29 = (bf16[128,128]{1,0:T(8,128)(2,1)S(1)}, bf16[128,128]{1,0:T(8,128)(2,1)S(1)}, u32[]{:S(2)}, u32[]{:S(2)}) collective-permute-start(bf16[128,128]{1,0:T(8,128)(2,1)S(1)} %slice_select_fusion), channel_id=1, source_target_pairs={{0,4},{4,0},{8,12},{12,8},{16,20},{20,16},{24,28},{28,24},{1,5},{5... | collective-permute-start | bytes 98312 | tf_op jit(solution)/shard_map/ppermute | solution.py:65
  (2 other events, 7.2 us)
